TPU v7x, 128 devices: a whole 4x4x4 slice. The times are simulated.
128 devices in a mesh: row: 8 (over x, z_lo), col: 16 (over y, z_hi, core).
Axes of the slice: x: 4, y: 4, z: 4 (z_hi: 2, z_lo: 2; z = z_hi * 2 + z_lo), core: 2. Of those that a mesh axis runs over, the one named last changes fastest.
Arguments:
- family_embedding: bfloat16 [128, 1024, 256], P('col', 'row'), may hold values from -6 to 6
- pairwise_embedding: bfloat16 [1024, 1024, 128], P('row', 'col'), may hold values from -6 to 6
- family_presence: int32 [128, 1024], P('col', 'row'), may hold values 0 or 1
- amino_validity: int32 [1024], replicated, may hold values from 0 to 1, as said below
- horizontal_query_projector: bfloat16 [4, 256, 256], replicated
- horizontal_final_projector: bfloat16 [256, 256], replicated, may hold values from -0.375 to 0.375
- pairwise_offset_factor: bfloat16 [128, 8], replicated, may hold values from -0.5 to 0.5
- vertical_query_projector: bfloat16 [4, 256, 256], replicated
- vertical_final_projector: bfloat16 [256, 256], replicated, may hold values from -0.375 to 0.375
- tensor_sided_projector: bfloat16 [2, 256, 32], replicated, may hold values from -0.375 to 0.375
- tensor_final_projector: bfloat16 [1024, 128], replicated, may hold values from -0.75 to 0.75
Outputs:
- alignment_output: bfloat16 [128, 1024, 256], P('col', 'row')
- pair_increment: bfloat16 [1024, 1024, 128], P('row', 'col')
Inputs may be any that keep to these rules, and one draw needn't show every extreme that they name: `amino_validity`: residues come in consecutive blocks of 64; each block ends with a padded tail of 0 to 32 zeros, and before that tail a residue may also be 0 (unresolved).
All inputs are finite; a program needn't handle non-finite values. No bound on the sum of `family_presence` on one device may be relied on, other than what follows from the above.
Results may differ from a plain program's by a relative error of at most 0.019.
Values may be sent and summed in bfloat16 or wider, within the bound.
A program may use at most 128 MiB of HBM per device.

v0:
```python
import math

import jax
import jax.numpy as jnp
from jax import lax
from jax.sharding import PartitionSpec as P

LAYER_EPS = 1e-05
MASK_BIG = 1000000000.0


def standardize_features(values_in):
    centred = values_in - jnp.mean(values_in, axis=-1, keepdims=True)
    spread = jnp.mean(centred * centred, axis=-1, keepdims=True)
    return centred * lax.rsqrt(spread + LAYER_EPS)


def affine_mapping(standardized_source, weight):
    return jnp.dot(standardized_source, weight, preferred_element_type=jnp.float32)


def softmax_rows(scores):
    highest = jnp.max(scores, axis=-1, keepdims=True)
    raised = jnp.exp(scores - highest)
    return raised / jnp.sum(raised, axis=-1, keepdims=True)


def per_device(
    family_embedding,
    pairwise_embedding,
    family_presence,
    amino_validity,
    horizontal_query_projector,
    horizontal_final_projector,
    pairwise_offset_factor,
    vertical_query_projector,
    vertical_final_projector,
    tensor_sided_projector,
    tensor_final_projector,
):
    homolog_overall, homolog_number, feature_number = family_embedding.shape
    head_count = pairwise_offset_factor.shape[1]
    head_width = horizontal_query_projector.shape[2]
    head_size = head_width // head_count
    inv_root = head_size ** (-0.5)
    offset = lax.axis_index("row") * homolog_number
    residue_present = lax.dynamic_slice_in_dim(amino_validity, offset, homolog_number, 0)
    present_mask = (family_presence * residue_present[None, :]).astype(jnp.float32)
    live_bf = present_mask.astype(jnp.bfloat16)
    standardized_source = standardize_features(family_embedding.astype(jnp.float32)).astype(
        jnp.bfloat16
    )
    query_rows = (
        affine_mapping(standardized_source, horizontal_query_projector[0]) * inv_root
    ).astype(jnp.bfloat16)
    horizontal_sigmoid_factor = jax.nn.sigmoid(
        affine_mapping(standardized_source, horizontal_query_projector[3])
    )
    normed_all, mask_all = (
        lax.all_gather(standardized_source, "row", axis=1, tiled=True),
        lax.all_gather(live_bf, "row", axis=1, tiled=True),
    )
    key_rows = affine_mapping(normed_all, horizontal_query_projector[1]).astype(jnp.bfloat16)
    value_rows = affine_mapping(normed_all, horizontal_query_projector[2]).astype(jnp.bfloat16)
    total_res = key_rows.shape[1]
    pair_normed = standardize_features(pairwise_embedding.astype(jnp.float32)).astype(jnp.bfloat16)
    bias_local = (
        affine_mapping(pair_normed, pairwise_offset_factor).astype(jnp.bfloat16).transpose(2, 0, 1)
    )
    bias_heads = lax.all_gather(bias_local, "col", axis=2, tiled=True).astype(jnp.float32)

    def row_one(pieces):
        query_one, key_one, value_one, mask_one = pieces
        scores = jnp.einsum(
            "ihd,jhd->hij",
            query_one.reshape(homolog_number, head_count, head_size),
            key_one.reshape(total_res, head_count, head_size),
            preferred_element_type=jnp.float32,
        )
        scores = jnp.where(
            mask_one.astype(jnp.float32)[None, None, :] > 0.5, scores + bias_heads, -MASK_BIG
        )
        weights = softmax_rows(scores).astype(jnp.bfloat16)
        attended = jnp.einsum(
            "hij,jhd->ihd",
            weights,
            value_one.reshape(total_res, head_count, head_size),
            preferred_element_type=jnp.float32,
        )
        return attended.reshape(homolog_number, head_width)

    horizontal_softmax_update = lax.map(row_one, (query_rows, key_rows, value_rows, mask_all))
    interim_family = (
        family_embedding.astype(jnp.float32)
        + affine_mapping(
            (horizontal_sigmoid_factor * horizontal_softmax_update).astype(jnp.bfloat16),
            horizontal_final_projector,
        )
    ).astype(jnp.bfloat16)
    peer_count = lax.axis_size("col")
    per_peer = homolog_number // peer_count
    family_blocked = interim_family.reshape(homolog_overall, peer_count, per_peer, feature_number)
    live_blocked = live_bf.reshape(homolog_overall, peer_count, per_peer)
    alignment_blocked = lax.all_to_all(
        family_blocked, "col", split_axis=1, concat_axis=0, tiled=True
    )
    mask_blocked = lax.all_to_all(live_blocked, "col", split_axis=1, concat_axis=0, tiled=True)
    alignment_columns = alignment_blocked[:, 0]
    column_mask = mask_blocked[:, 0]
    every_sequence = alignment_columns.shape[0]
    residue_entries = alignment_columns.shape[1]
    normalized_between = standardize_features(alignment_columns.astype(jnp.float32)).astype(
        jnp.bfloat16
    )
    query_cols = (
        affine_mapping(normalized_between, vertical_query_projector[0]) * inv_root
    ).astype(jnp.bfloat16)
    key_cols = affine_mapping(normalized_between, vertical_query_projector[1]).astype(jnp.bfloat16)
    value_cols = affine_mapping(normalized_between, vertical_query_projector[2]).astype(
        jnp.bfloat16
    )
    column_gate = jax.nn.sigmoid(affine_mapping(normalized_between, vertical_query_projector[3]))
    shaped = (every_sequence, residue_entries, head_count, head_size)
    scores = jnp.einsum(
        "sbhd,tbhd->bhst",
        query_cols.reshape(shaped),
        key_cols.reshape(shaped),
        preferred_element_type=jnp.float32,
    )
    mask_cols = column_mask.astype(jnp.float32).T
    scores = jnp.where(mask_cols[:, None, None, :] > 0.5, scores, -MASK_BIG)
    weights = softmax_rows(scores).astype(jnp.bfloat16)
    attended = jnp.einsum(
        "bhst,tbhd->sbhd", weights, value_cols.reshape(shaped), preferred_element_type=jnp.float32
    ).reshape(every_sequence, residue_entries, head_width)
    pair_delta = affine_mapping(
        (column_gate * attended).astype(jnp.bfloat16), vertical_final_projector
    )
    updated = (alignment_columns.astype(jnp.float32) + pair_delta).astype(jnp.bfloat16)
    column_output = updated[:, None]
    returned = lax.all_to_all(column_output, "col", split_axis=0, concat_axis=1, tiled=True)
    alignment_output = returned.reshape(homolog_overall, homolog_number, feature_number)
    normalized_output = standardize_features(alignment_output.astype(jnp.float32)).astype(
        jnp.bfloat16
    )
    left_local = (
        (affine_mapping(normalized_output, tensor_sided_projector[0]) * present_mask[:, :, None])
        .astype(jnp.bfloat16)
        .transpose(0, 2, 1)
    )
    right_local = (
        (affine_mapping(normalized_output, tensor_sided_projector[1]) * present_mask[:, :, None])
        .astype(jnp.bfloat16)
        .transpose(0, 2, 1)
    )
    mask_three = live_bf[:, None, :]
    left_all, left_mask = (
        lax.all_gather(left_local, "col", axis=0, tiled=True),
        lax.all_gather(mask_three, "col", axis=0, tiled=True),
    )
    right_rows, right_mask_rows = (
        lax.all_gather(right_local, "row", axis=2, tiled=True),
        lax.all_gather(mask_three, "row", axis=2, tiled=True),
    )
    right_all, right_mask = (
        lax.all_to_all(right_rows, "col", split_axis=2, concat_axis=0, tiled=True),
        lax.all_to_all(right_mask_rows, "col", split_axis=2, concat_axis=0, tiled=True),
    )
    every_sequence = left_all.shape[0]
    out_channels = left_all.shape[1]
    col_width = right_all.shape[2]
    pair_count = jnp.dot(
        left_mask[:, 0, :].T, right_mask[:, 0, :], preferred_element_type=jnp.float32
    )
    block_rows = math.gcd(homolog_number, 16)
    left_blocks = left_all.reshape(
        every_sequence, out_channels, homolog_number // block_rows, block_rows
    ).transpose(2, 0, 1, 3)

    def opm_block(left_one):
        outer = jnp.einsum("sci,sdj->icdj", left_one, right_all, preferred_element_type=jnp.float32)
        outer = outer.astype(jnp.bfloat16).reshape(
            block_rows, out_channels * out_channels, col_width
        )
        return jnp.einsum(
            "ikj,kz->ijz", outer, tensor_final_projector, preferred_element_type=jnp.float32
        )

    summed = lax.map(opm_block, left_blocks).reshape(
        homolog_number, col_width, tensor_final_projector.shape[1]
    )
    pair_increment = (summed / jnp.maximum(pair_count, 1.0)[:, :, None]).astype(jnp.bfloat16)
    return (alignment_output, pair_increment)


def solution(mesh):
    in_specs = (
        P("col", "row", None),
        P("row", "col", None),
        P("col", "row"),
        P(),
        P(),
        P(),
        P(),
        P(),
        P(),
        P(),
        P(),
    )
    out_specs = (P("col", "row", None), P("row", "col", None))
    return jax.shard_map(
        per_device, mesh=mesh, in_specs=in_specs, out_specs=out_specs, check_vma=False
    )
```

profile of v0, /device:TPU:1, one launch (start us, length us, event | category | flops | bytes accessed | tf_op | source)
XLA Modules:
  0.0 451.5 jit_solution(4113636795161841731)
XLA Ops:
  21.5 9.3 %all-to-all-start.1 = ((bf16[8,16,8]{2,0,1:T(8,128)(2,1)}), bf16[8,16,8]{2,0,1:T(8,128)(2,1)S(1)}, u32[]{:S(2)}, u32[]{:S(2)}) async-start(bf16[8,16,8]{2,0,1:T(8,128)(2,1)} %copy.93), calls=%async_computation.1 | async-start | bytes 65536 | tf_op jit(solution)/shard_map/all_to_all | solution.py:107
  30.8 20.3 %all_gather.22 = bf16[8,1024]{1,0:T(8,128)(2,1)S(1)} all-gather(bf16[8,128]{1,0:T(8,128)(2,1)S(1)} %get-tuple-element.121), channel_id=1, replica_groups=mesh['row'=8,'col'=16] {'row'}, dimensions={1}, use_global_device_ids=true | all-gather | bytes 18432 | tf_op jit(solution)/shard_map/all_gather | solution.py:61
  52.5 17.9 %all-gather.8.cloned.1.call-done = bf16[8,128,1024]{1,0,2:T(8,128)(2,1)} async-done(((bf16[8,128,64]{1,0,2:T(8,128)(2,1)}), bf16[8,128,1024]{1,0,2:T(8,128)(2,1)}) %all-gather.8.cloned.1.call-update) | async-done | bytes 2097168 | tf_op jit(solution)/shard_map/all_gather | solution.py:70
  70.4 4.7 %copy.86 = f32[8,128,1024]{2,1,0:T(8,128)} copy(bf16[8,128,1024]{1,0,2:T(8,128)(2,1)} %all-gather.8.cloned.1.call-done) | data formatting | bytes 6291456 | tf_op jit(solution)/shard_map/while | solution.py:92
  75.1 85.5 %all-gather.6.cloned.1.call-done = bf16[8,1024,256]{2,1,0:T(8,128)(2,1)} async-done(((bf16[8,128,256]{2,1,0:T(8,128)(2,1)}), bf16[8,1024,256]{2,1,0:T(8,128)(2,1)}) %all-gather.6.cloned.1.call-update) | async-done | bytes 4194320 | tf_op jit(solution)/shard_map/all_gather | solution.py:60
  160.6 5.6 %convolution_convert_fusion.1 = bf16[8,1024,256]{2,1,0:T(8,128)(2,1)} fusion(bf16[8,1024,256]{2,1,0:T(8,128)(2,1)} %all-gather.6.cloned.1.call-done, bf16[4,256,256]{2,1,0:T(8,128)(2,1)S(1)} %copy-done.5), kind=kOutput, calls=%fused_computation.34 | convolution fusion | flops 1075838976 | bytes 8519680 | tf_op jit(solution)/shard_map/dot_general | solution.py:19
  169.4 111.9 %while.20 = (s32[]{:T(128)}, f32[8,128,256]{2,1,0:T(8,128)}, bf16[8,1024,256]{2,1,0:T(8,128)(2,1)}, bf16[8,1024]{1,0:T(8,128)(2,1)S(1)}, bf16[8,128,256]{2,1,0:T...) while((s32[]{:T(128)}, f32[8,128,256]{2,1,0:T(8,128)}, ...), condition=%wide.region_7.8_spmd, body=%wide.region_4.7_spmd.sunk | while | flops 141562880 | bytes 39793276 | solution.py:92
  177.2 5.4 %fusion.154 = f32[8,32,128]{2,1,0:T(8,128)S(1)} fusion(bf16[1024,8,32]{0,2,1:T(8,128)(2,1)S(1)} %bitcast.194, f32[8,128]{1,0:T(8,128)S(1)} %fusion.153, f32[8,128,1024]{2,1,0:T(8,128)} %copy-done.1), kind=kOutput, calls=%fused_computation.14.clone.1 | convolution fusion | flops 70256640 | bytes 4853760 | tf_op jit(solution)/shard_map/while/body/eval_jaxpr/hij,jhd->ihd/dot_general | solution.py:84
  191.2 5.4 %fusion.154 = f32[8,32,128]{2,1,0:T(8,128)S(1)} fusion(bf16[1024,8,32]{0,2,1:T(8,128)(2,1)S(1)} %bitcast.194, f32[8,128]{1,0:T(8,128)S(1)} %fusion.153, f32[8,128,1024]{2,1,0:T(8,128)} %copy-done.1), kind=kOutput, calls=%fused_computation.14.clone.1 | convolution fusion | flops 70256640 | bytes 4853760 | tf_op jit(solution)/shard_map/while/body/eval_jaxpr/hij,jhd->ihd/dot_general | solution.py:84
  205.2 5.4 %fusion.154 = f32[8,32,128]{2,1,0:T(8,128)S(1)} fusion(bf16[1024,8,32]{0,2,1:T(8,128)(2,1)S(1)} %bitcast.194, f32[8,128]{1,0:T(8,128)S(1)} %fusion.153, f32[8,128,1024]{2,1,0:T(8,128)} %copy-done.1), kind=kOutput, calls=%fused_computation.14.clone.1 | convolution fusion | flops 70256640 | bytes 4853760 | tf_op jit(solution)/shard_map/while/body/eval_jaxpr/hij,jhd->ihd/dot_general | solution.py:84
  219.2 5.4 %fusion.154 = f32[8,32,128]{2,1,0:T(8,128)S(1)} fusion(bf16[1024,8,32]{0,2,1:T(8,128)(2,1)S(1)} %bitcast.194, f32[8,128]{1,0:T(8,128)S(1)} %fusion.153, f32[8,128,1024]{2,1,0:T(8,128)} %copy-done.1), kind=kOutput, calls=%fused_computation.14.clone.1 | convolution fusion | flops 70256640 | bytes 4853760 | tf_op jit(solution)/shard_map/while/body/eval_jaxpr/hij,jhd->ihd/dot_general | solution.py:84
  233.1 5.4 %fusion.154 = f32[8,32,128]{2,1,0:T(8,128)S(1)} fusion(bf16[1024,8,32]{0,2,1:T(8,128)(2,1)S(1)} %bitcast.194, f32[8,128]{1,0:T(8,128)S(1)} %fusion.153, f32[8,128,1024]{2,1,0:T(8,128)} %copy-done.1), kind=kOutput, calls=%fused_computation.14.clone.1 | convolution fusion | flops 70256640 | bytes 4853760 | tf_op jit(solution)/shard_map/while/body/eval_jaxpr/hij,jhd->ihd/dot_general | solution.py:84
  247.1 5.4 %fusion.154 = f32[8,32,128]{2,1,0:T(8,128)S(1)} fusion(bf16[1024,8,32]{0,2,1:T(8,128)(2,1)S(1)} %bitcast.194, f32[8,128]{1,0:T(8,128)S(1)} %fusion.153, f32[8,128,1024]{2,1,0:T(8,128)} %copy-done.1), kind=kOutput, calls=%fused_computation.14.clone.1 | convolution fusion | flops 70256640 | bytes 4853760 | tf_op jit(solution)/shard_map/while/body/eval_jaxpr/hij,jhd->ihd/dot_general | solution.py:84
  261.1 5.4 %fusion.154 = f32[8,32,128]{2,1,0:T(8,128)S(1)} fusion(bf16[1024,8,32]{0,2,1:T(8,128)(2,1)S(1)} %bitcast.194, f32[8,128]{1,0:T(8,128)S(1)} %fusion.153, f32[8,128,1024]{2,1,0:T(8,128)} %copy-done.1), kind=kOutput, calls=%fused_computation.14.clone.1 | convolution fusion | flops 70256640 | bytes 4853760 | tf_op jit(solution)/shard_map/while/body/eval_jaxpr/hij,jhd->ihd/dot_general | solution.py:84
  275.1 5.4 %fusion.154 = f32[8,32,128]{2,1,0:T(8,128)S(1)} fusion(bf16[1024,8,32]{0,2,1:T(8,128)(2,1)S(1)} %bitcast.194, f32[8,128]{1,0:T(8,128)S(1)} %fusion.153, f32[8,128,1024]{2,1,0:T(8,128)} %copy-done.1), kind=kOutput, calls=%fused_computation.14.clone.1 | convolution fusion | flops 70256640 | bytes 4853760 | tf_op jit(solution)/shard_map/while/body/eval_jaxpr/hij,jhd->ihd/dot_general | solution.py:84
  284.1 7.3 %all-to-all-start = ((bf16[8,16,8,256]{3,2,0,1:T(8,128)(2,1)}), bf16[8,16,8,256]{3,2,0,1:T(8,128)(2,1)S(1)}, u32[]{:S(2)}, u32[]{:S(2)}) async-start(bf16[8,16,8,256]{3,2,0,1:T(8,128)(2,1)} %copy.88), calls=%async_computation | async-start | bytes 1048576 | tf_op jit(solution)/shard_map/all_to_all | solution.py:104
  291.8 10.8 %all-to-all-done = bf16[8,16,8,256]{3,2,0,1:T(8,128)(2,1)S(1)} async-done(((bf16[8,16,8,256]{3,2,0,1:T(8,128)(2,1)}), bf16[8,16,8,256]{3,2,0,1:T(8,128)(2,1)S(1)}, u32[]{:S(2)}, u32[]{:S(2)}) %all-to-all-start) | async-done | bytes 524320 | tf_op jit(solution)/shard_map/all_to_all | solution.py:104
  307.0 4.6 %fusion.118 = (f32[8,8,128]{2,1,0:T(8,128)S(1)}, f32[8,8,128,128]{2,3,1,0:T(8,128)}) fusion(pred[8,128]{1,0:T(8,128)(4,1)S(1)} %bitcast.219, bf16[128,8,8,32]{0,3,2,1:T(8,128)(2,1)S(1)} %bitcast.214, bf16[128,8,8,32]{0,3,2,1:T(8,128)(2,1)} %bitcast.216), kind=kOutput, calls=%fused_computation.144 | convolution fusion | flops 70254720 | bytes 5276672 | tf_op jit(solution)/shard_map/sub | solution.py:24
  316.9 15.0 %all_to_all.66 = bf16[128,1,8,256]{3,2,1,0:T(8,128)(2,1)S(1)} all-to-all(bf16[128,1,8,256]{3,2,1,0:T(8,128)(2,1)S(1)} %copy.101), channel_id=1, replica_groups=mesh['row'=8,'col'=16] {'col'}, dimensions={0} | all-to-all | bytes 1048576 | tf_op jit(solution)/shard_map/all_to_all | solution.py:141
  337.7 4.6 %all-to-all-start.4 = ((bf16[16,2,256]{2,1,0:T(2,128)(2,1)}), bf16[16,2,256]{2,1,0:T(2,128)(2,1)S(1)}, u32[]{:S(2)}, u32[]{:S(2)}) async-start(bf16[16,2,256]{2,1,0:T(2,128)(2,1)} %reshape.225), calls=%async_computation.4 | async-start | bytes 32768 | tf_op jit(solution)/shard_map/all_to_all | solution.py:167
  342.8 22.7 %all_gather.25 = bf16[8,32,1024]{2,1,0:T(8,128)(2,1)S(1)} all-gather(bf16[8,32,128]{2,1,0:T(8,128)(2,1)S(1)} %fusion.60), channel_id=1, replica_groups=mesh['row'=8,'col'=16] {'row'}, dimensions={2}, use_global_device_ids=true | all-gather | bytes 589824 | tf_op jit(solution)/shard_map/all_gather | solution.py:162
  369.7 12.0 %all-to-all-start.3 = ((bf16[16,2,8192]{2,1,0:T(2,128)(2,1)}), bf16[16,2,8192]{2,1,0:T(2,128)(2,1)S(1)}, u32[]{:S(2)}, u32[]{:S(2)}) async-start(bf16[16,2,8192]{2,1,0:T(2,128)(2,1)} %reshape.223), calls=%async_computation.3 | async-start | bytes 1048576 | tf_op jit(solution)/shard_map/all_to_all | solution.py:166
  381.7 24.7 %all-gather = bf16[128,128]{1,0:T(8,128)(2,1)S(1)} all-gather(bf16[8,128]{1,0:T(8,128)(2,1)S(1)} %get-tuple-element.121), channel_id=2, replica_groups=mesh['row'=8,'col'=16] {'col'}, dimensions={0}, use_global_device_ids=true | all-gather | bytes 34816 | tf_op jit(solution)/shard_map/all_gather | solution.py:159
  414.0 27.2 %while.21 = (s32[]{:T(128)}, f32[8,16,64,128]{3,2,1,0:T(8,128)}, bf16[8,128,32,16]{1,3,0,2:T(8,128)(2,1)S(1)}, bf16[128,32,64]{0,2,1:T(8,128)(2,1)S(1)}, bf16[1024,128]{1,0:T(8,128)(2,1)}, /*index=5*/s32[]{:T(128)}) while((s32[]{:T(128)}, f32[8,16,64,128]{3,2,1,0:T(8,128)}, bf16[8,128,32,16]{1,3,0,2:T(8,128)(2,1)S(1)}, ...), condition=%wide.region_15.16_spmd, body=%wide.region_14.15_spmd.sunk | while | flops 537919488 | bytes 6685285 | solution.py:189
  (220 shorter events, 148.4 us)
Async XLA Ops:
  7.2 274.2 %copy-start = (bf16[256,256]{1,0:T(8,128)(2,1)S(1)}, bf16[256,256]{1,0:T(8,128)(2,1)}, u32[]{:S(2)}) copy-start(bf16[256,256]{1,0:T(8,128)(2,1)} %param.20) | copy-start | bytes 393220
  7.2 7.1 %copy-start.3 = (bf16[128,64,128]{2,1,0:T(8,128)(2,1)S(1)}, bf16[128,64,128]{2,1,0:T(8,128)(2,1)}, u32[]{:S(2)}) copy-start(bf16[128,64,128]{2,1,0:T(8,128)(2,1)} %param.16) | copy-start | bytes 6291460
  7.2 7.1 %copy-start.11 = (bf16[128,8]{0,1:T(8,128)(2,1)S(1)}, bf16[128,8]{0,1:T(8,128)(2,1)}, u32[]{:S(2)}) copy-start(bf16[128,8]{0,1:T(8,128)(2,1)} %param.21) | copy-start | bytes 6148
  7.2 10.9 %copy-start.4 = (bf16[8,128,256]{2,1,0:T(8,128)(2,1)S(1)}, bf16[8,128,256]{2,1,0:T(8,128)(2,1)}, u32[]{:S(2)}) copy-start(bf16[8,128,256]{2,1,0:T(8,128)(2,1)} %param.15) | copy-start | bytes 1572868
  7.2 63.2 %all-gather.8.cloned.1.call-start = ((), (), s32[]{:S(2)}) async-start(), calls=%async_computation.6 | async-start | bytes 2228224 | tf_op jit(solution)/shard_map/all_gather | solution.py:70
  14.2 6.5 %copy-start.7 = (s32[8,128]{1,0:T(8,128)S(1)}, s32[8,128]{1,0:T(8,128)}, u32[]{:S(2)}) copy-start(s32[8,128]{1,0:T(8,128)} %param.17) | copy-start | bytes 12292
  18.1 142.6 %all-gather.6.cloned.1.call-start = ((), (), s32[]{:S(2)}) async-start(), calls=%async_computation.5 | async-start | bytes 4718592 | tf_op jit(solution)/shard_map/all_gather | solution.py:60
  19.9 140.7 %copy-start.5 = (bf16[4,256,256]{2,1,0:T(8,128)(2,1)S(1)}, bf16[4,256,256]{2,1,0:T(8,128)(2,1)}, u32[]{:S(2)}) copy-start(bf16[4,256,256]{2,1,0:T(8,128)(2,1)} %param.19) | copy-start | bytes 1572868
  21.5 262.6 %all-to-all-start.1 = ((bf16[8,16,8]{2,0,1:T(8,128)(2,1)}), bf16[8,16,8]{2,0,1:T(8,128)(2,1)S(1)}, u32[]{:S(2)}, u32[]{:S(2)}) async-start(bf16[8,16,8]{2,0,1:T(8,128)(2,1)} %copy.93), calls=%async_computation.1 | async-start | bytes 65536 | tf_op jit(solution)/shard_map/all_to_all | solution.py:107
  160.6 5.6 %copy-start.2 = (bf16[8,1024,256]{2,1,0:T(8,128)(2,1)S(1)}, bf16[8,1024,256]{2,1,0:T(8,128)(2,1)}, u32[]{:S(2)}) copy-start(bf16[8,1024,256]{2,1,0:T(8,128)(2,1)} %all-gather.6.cloned.1.call-done) | copy-start | bytes 12582916
  174.0 2.0 copy-start.1
  188.0 2.0 copy-start.1
  202.0 2.0 copy-start.1
  216.0 2.0 copy-start.1
  230.0 2.0 copy-start.1
  244.0 2.0 copy-start.1
  258.0 2.0 copy-start.1
  281.3 22.2 %copy-start.6 = (bf16[4,256,256]{2,1,0:T(8,128)(2,1)S(1)}, bf16[4,256,256]{2,1,0:T(8,128)(2,1)}, u32[]{:S(2)}) copy-start(bf16[4,256,256]{2,1,0:T(8,128)(2,1)} %param.22) | copy-start | bytes 1572868
  284.1 18.4 %all-to-all-start = ((bf16[8,16,8,256]{3,2,0,1:T(8,128)(2,1)}), bf16[8,16,8,256]{3,2,0,1:T(8,128)(2,1)S(1)}, u32[]{:S(2)}, u32[]{:S(2)}) async-start(bf16[8,16,8,256]{3,2,0,1:T(8,128)(2,1)} %copy.88), calls=%async_computation | async-start | bytes 1048576 | tf_op jit(solution)/shard_map/all_to_all | solution.py:104
  291.4 120.6 %all-gather.10.cloned.1.call-start = ((), (), s32[]{:S(2)}) async-start(), calls=%async_computation.7 | async-start | bytes 1114112 | tf_op jit(solution)/shard_map/all_gather | solution.py:158
  311.6 3.3 copy-start.9
  315.0 17.5 %copy-start.10 = (bf16[2,256,32]{1,2,0:T(8,128)(2,1)S(1)}, bf16[2,256,32]{1,2,0:T(8,128)(2,1)}, u32[]{:S(2)}) copy-start(bf16[2,256,32]{1,2,0:T(8,128)(2,1)} %param.24) | copy-start | bytes 98308
  337.7 32.1 %all-to-all-start.4 = ((bf16[16,2,256]{2,1,0:T(2,128)(2,1)}), bf16[16,2,256]{2,1,0:T(2,128)(2,1)S(1)}, u32[]{:S(2)}, u32[]{:S(2)}) async-start(bf16[16,2,256]{2,1,0:T(2,128)(2,1)} %reshape.225), calls=%async_computation.4 | async-start | bytes 32768 | tf_op jit(solution)/shard_map/all_to_all | solution.py:167
  369.7 38.9 %all-to-all-start.3 = ((bf16[16,2,8192]{2,1,0:T(2,128)(2,1)}), bf16[16,2,8192]{2,1,0:T(2,128)(2,1)S(1)}, u32[]{:S(2)}, u32[]{:S(2)}) async-start(bf16[16,2,8192]{2,1,0:T(2,128)(2,1)} %reshape.223), calls=%async_computation.3 | async-start | bytes 1048576 | tf_op jit(solution)/shard_map/all_to_all | solution.py:166
  (9 other events, 12.2 us)
Sparse Core Ops, SparseCore 0:
  18.2 52.1 all-gather.7
  72.6 87.9 all-gather.5
  333.7 45.9 all-gather.9
where the time goes:
time: 453 us; the launch traced here: 452 us
  matrix products  122 us (27%)
  waiting for transfers between devices  114 us (25%)
  blocking collectives  82.6 us (18%)
  local copies, waits for them, and re-layouts  60 us (13%)
  starting transfers between devices  33.5 us (7%)
  other arithmetic  24.6 us (5%)
  between operations  14.2 us (3%)
    all_gather x1, waiting for transfers between devices, per_device(): lax.all_gather(standardized_source, 'row', axis=1, tiled=True)  85.5 us
    dot_general x8, matrix products, row_one(): jnp.einsum('hij,jhd->ihd', weights, value_one.reshape(total_res, head_cou...  43.4 us
    all_gather x1, blocking collectives, per_device(): lax.all_gather(mask_three, 'col', axis=0, tiled=True)  24.7 us
    dot_general x8, matrix products, row_one(): jnp.einsum('ihd,jhd->hij', query_one.reshape(homolog_number, head_count,...  23.5 us
    all_gather x1, blocking collectives, per_device(): lax.all_gather(right_local, 'row', axis=2, tiled=True)  22.7 us
    all_gather x1, blocking collectives, per_device(): lax.all_gather(live_bf, 'row', axis=1, tiled=True)  20.3 us
    dot_general x11, matrix products, affine_mapping(): jnp.dot(standardized_source, weight, preferred_element_type=jnp.float32)  20 us
    all_gather x1, waiting for transfers between devices, per_device(): lax.all_gather(bias_local, 'col', axis=2, tiled=True).astype(jnp.float32)  17.9 us
  transfers between devices with their start and end apart: 7, of which 3 were waited for; matrix products, arithmetic and copies ran while one was open for 29% of the time, Pallas kernels for 0%

commit v1 on v0

v1 whole, which is shorter than its diff:
```python
import jax
import jax.numpy as jnp
from jax import lax
from jax.experimental import pallas as pl
from jax.experimental.pallas import tpu as pltpu
from jax.sharding import PartitionSpec as P

BF = jnp.bfloat16
F32 = jnp.float32
EPS = 1e-05
MASK_BIG = 1000000000.0
MESH = pl.DeviceIdType.MESH

NR = 8
NC = 16
S = 8
R = 128
D = 256
H = 8
HD = 32
G = 4
HP = 2


def norm(x):
    c = x - jnp.mean(x, axis=-1, keepdims=True)
    return c * lax.rsqrt(jnp.mean(c * c, axis=-1, keepdims=True) + EPS)


def dot(a, b):
    return jnp.dot(a, b, preferred_element_type=F32)


def dot_t(a, b):
    return lax.dot_general(a, b, (((1,), (1,)), ((), ())), preferred_element_type=F32)


def sigmoid(x):
    return 1.0 / (1.0 + jnp.exp(-x))


def head_lanes(rows):
    return lax.broadcasted_iota(jnp.int32, (rows, D), 1) // HD


def attend(q, k, v, score_of):
    n = q.shape[0]
    lanes = head_lanes(n)
    total = jnp.zeros((n, D), F32)
    for h0 in range(0, H, HP):
        heads = range(h0, h0 + HP)
        stacked = jnp.concatenate([jnp.where(lanes == h, q, jnp.zeros_like(q)) for h in heads], axis=0)
        raw = dot_t(stacked, k)
        parts, sums = [], []
        for at, h in enumerate(heads):
            s = score_of(h, raw[at * n:(at + 1) * n])
            p = jnp.exp(s - jnp.max(s, axis=-1, keepdims=True))
            sums.append(jnp.sum(p, axis=-1, keepdims=True))
            parts.append(p.astype(BF))
        out = dot(jnp.concatenate(parts, axis=0), v)
        for at, h in enumerate(heads):
            total = jnp.where(lanes == h, out[at * n:(at + 1) * n] * (1.0 / sums[at]), total)
    return total


def msa_kernel(
    fam, pair, present, valid, wh, wo, wb, wv, wvo, wlr,
    align, lt_out, rt_out, inv_out,
    nall, live, bscr, mine, sib, ball, qs, gs, ks, vs, midf, snd, rcv,
    xf, nf, upf, back_snd, back_rcv, lf, rf, lsnd, lrcv, rsnd, rrcv, ltt, cmask,
    n_s, n_r, lv_s, lv_r, lc_s, lc_r, sb_s, sb_r, b_s, b_r, bc_s, bc_r,
    m_s, m_r, u_s, u_r, le_s, le_r, ri_s, ri_r,
):
    r = lax.axis_index("row")
    c = lax.axis_index("col")
    core = lax.rem(c, 2)
    blk = c // 2

    def flip(i):
        return i + 1 - 2 * lax.rem(i, 2)

    def copy(src, dst, ss, rs, row, col):
        return pltpu.make_async_remote_copy(
            src_ref=src, dst_ref=dst, send_sem=ss, recv_sem=rs, device_id=(row, col), device_id_type=MESH
        )

    rz, rl, rr, rf2 = flip(r), lax.rem(r + 6, 8), lax.rem(r + 2, 8), lax.rem(r + 4, 8)

    def ncopy(g, slot, block, lo, n, to):
        ref = nall.at[block, pl.ds(2 * g + lo, n)]
        return copy(ref, ref, n_s.at[g, slot], n_r.at[g, slot], to, c)

    n_plan = [
        (r, 0, 2, rz), (r, 0, 2, rr), (r, 0, 2, rl), (rz, 0, 2, rr), (rz, 0, 2, rl),
        (rl, 0, 1, rr), (rr, 1, 1, rl), (rf2, 0, 2, rz),
    ]

    def n_slot(g, i):
        return ncopy(g, i, *n_plan[i])

    def n1(g):
        for i in (0, 1, 2):
            n_slot(g, i).start()

    def n2(g):
        for i in (0, 1, 2):
            n_slot(g, i).wait_recv()
        for i in (3, 4, 5, 6):
            n_slot(g, i).start()

    def n3(g):
        for i in (5, 6):
            n_slot(g, i).wait_recv()
        n_slot(g, 7).start()

    def n4(g):
        for i in (3, 4, 7):
            n_slot(g, i).wait_recv()

    h0 = core * 4
    cz, cl, cr, cs = c + 2 - 4 * lax.rem(blk, 2), lax.rem(c + 12, 16), lax.rem(c + 4, 16), flip(c)
    bz, bl, br, bf2 = flip(blk), lax.rem(blk + 6, 8), lax.rem(blk + 2, 8), lax.rem(blk + 4, 8)

    def bcopy(slot, block, lo, n, to):
        ref = ball.at[block, pl.ds(h0 + lo, n)]
        return copy(ref, ref, b_s.at[slot], b_r.at[slot], r, to)

    b_slots = [
        bcopy(0, blk, 0, 4, cz), bcopy(1, blk, 0, 4, cr), bcopy(2, blk, 0, 4, cl),
        bcopy(3, bz, 0, 4, cr), bcopy(4, bz, 0, 4, cl),
        bcopy(5, bl, 0, 2, cr), bcopy(6, br, 2, 2, cl), bcopy(7, bf2, 0, 4, cz),
    ]

    def bcore(slot, block):
        ref = ball.at[block, pl.ds(h0, 4)]
        return copy(ref, ref, bc_s.at[slot], bc_r.at[slot], r, cs)

    bc_slots = [
        bcore(0, bz), bcore(1, bl), bcore(2, br), bcore(3, flip(bl)), bcore(4, flip(br)),
        bcore(5, bf2), bcore(6, flip(bf2)),
    ]

    for s in range(S):
        nall[r, s] = norm(fam[s].astype(F32)).astype(BF)
    live[c, r] = (present[...] * valid[pl.ds(r, 1), :]).astype(F32)
    n1(0)
    n1(1)

    def lv(k):
        ref = live.at[c, r]
        return copy(ref, ref, lv_s.at[k], lv_r.at[k], lax.rem(r + k, 8), c)

    for k in range(1, 8):
        lv(k).start()

    def bias_step(t, carry):
        lo = pair[pl.ds(t * 8, 8)].astype(F32)
        hi = pair[pl.ds(64 + t * 8, 8)].astype(F32)
        x = norm(jnp.concatenate([lo, hi], axis=1).reshape(1024, 128)).astype(BF)
        b = dot_t(wb[...], x)
        for i in range(8):
            bscr[pl.ds(t * 64 + i * 8, 8), :] = b[:, i * 128:(i + 1) * 128]
        return carry

    lax.fori_loop(0, 8, bias_step, 0)
    for h in range(H):
        mine[h] = bscr[pl.ds(h, 64, stride=8), :].astype(BF)
    sib_copy = copy(mine, sib, sb_s, sb_r, r, cs)
    sib_copy.start()
    n2(0)
    n1(2)

    def qg_step(s, carry):
        x = nall[r, s]
        qs[s] = (dot(x, wh[0]) * (HD ** -0.5)).astype(BF)
        gs[s] = sigmoid(dot(x, wh[3]))
        return carry

    lax.fori_loop(0, S, qg_step, 0)

    sib_copy.wait_recv()
    low = lax.broadcasted_iota(jnp.int32, (64, 128), 1) < 64
    for h in range(H):
        a = mine[h].astype(F32)
        b = sib[h].astype(F32)
        first = jnp.where(core == 0, a, b)
        second = jnp.where(core == 0, b, a)
        ball[blk, h, 0:64, :] = jnp.where(low, first, pltpu.roll(second, 64, 1)).astype(BF)
        ball[blk, h, 64:128, :] = jnp.where(low, pltpu.roll(first, 64, 1), second).astype(BF)
    for i in (0, 1, 2):
        b_slots[i].start()
    n2(1)
    n3(0)
    for k in range(1, 8):
        lv(k).wait_recv()

    def lc(k):
        ref = live.at[c]
        return copy(ref, ref, lc_s.at[k], lc_r.at[k], r, lax.rem(c + k, 16))

    for k in range(1, 16):
        lc(k).start()
    for i in (0, 1, 2):
        b_slots[i].wait_recv()
    for i in (3, 4, 5, 6):
        b_slots[i].start()
    for i in (0, 1, 2):
        bc_slots[i].start()
    for i in (5, 6):
        b_slots[i].wait_recv()
    b_slots[7].start()
    bc_slots[5].start()
    for i in (3, 4):
        b_slots[i].wait_recv()
    for i in (3, 4):
        bc_slots[i].start()
    b_slots[7].wait_recv()
    bc_slots[6].start()
    for i in range(7):
        bc_slots[i].wait_recv()

    def mcopy(g, k):
        to = lax.rem(c + k, 16)
        rows = pl.ds(g * 16, 16)
        return copy(snd.at[to, rows], rcv.at[c, rows], m_s.at[g, k], m_r.at[g, k], r, to)

    def group(g, carry):
        @pl.when(g < G - 3)
        def _():
            n1(g + 3)

        @pl.when(g < G - 2)
        def _():
            n2(g + 2)

        @pl.when(g < G - 1)
        def _():
            n3(g + 1)

        n4(g)

        def row_one(i, carry):
            s = 2 * g + i
            for b in range(NR):
                x = nall[b, s]
                ks[b * R:(b + 1) * R, :] = dot(x, wh[1]).astype(BF)
                vs[b * R:(b + 1) * R, :] = dot(x, wh[2]).astype(BF)
            keep = jnp.concatenate([live[c, b, pl.ds(s, 1), :] for b in range(NR)], axis=1) > 0.5

            def score(h, raw):
                bias = jnp.concatenate([ball[b, h] for b in range(NR)], axis=1)
                return jnp.where(keep, raw + bias.astype(F32), -MASK_BIG)

            o = attend(qs[s], ks[...], vs[...], score)
            gated = (gs[s] * o).astype(BF)
            midf[i] = fam[s].astype(F32) + dot(gated, wo[...])
            return carry

        lax.fori_loop(0, 2, row_one, 0)
        for t in range(NC):
            two = jnp.concatenate([midf[0, t * 8:(t + 1) * 8, :], midf[1, t * 8:(t + 1) * 8, :]], axis=0)
            snd[t, pl.ds(pl.multiple_of(g * 16, 16), 16), :] = two.astype(BF)
        for k in range(1, 16):
            mcopy(g, k).start()
        return carry

    lax.fori_loop(0, G, group, 0)
    rcv[c] = snd[c]
    for k in range(1, 16):
        lc(k).wait_recv()
    by_res = live[:, r].reshape(R, R).T
    cmask[...] = by_res
    by_col = live[:, blk].reshape(R, R).T
    ltt[...] = by_col
    right_live = ltt[pl.ds(pl.multiple_of(core * 64, 64), 64), :]
    inv_out[...] = 1.0 / jnp.maximum(dot_t(right_live.astype(BF), by_res.astype(BF)), 1.0)
    for g in range(G):
        for k in range(1, 16):
            mcopy(g, k).wait_recv()

    def col_norm(t, carry):
        x = rcv[t].astype(F32)
        rows = pl.ds(pl.multiple_of(t * 64, 64), 64)
        y = norm(x)
        for i in range(2):
            xf[i, rows, :] = x[:, i * 128:(i + 1) * 128]
            nf[i, rows, :] = y[:, i * 128:(i + 1) * 128]
        return carry

    lax.fori_loop(0, NC, col_norm, 0)

    def col_one(b, carry):
        every = pl.ds(b, R, stride=8)
        x = jnp.concatenate([nf[i, every, :] for i in range(2)], axis=1).astype(BF)
        q = (dot(x, wv[0]) * (HD ** -0.5)).astype(BF)
        k = dot(x, wv[1]).astype(BF)
        v = dot(x, wv[2]).astype(BF)
        gate = sigmoid(dot(x, wv[3]))
        row = cmask[pl.ds(c * 8 + b, 1), :]

        def score(h, raw):
            return jnp.where(row > 0.5, raw, -MASK_BIG)

        o = attend(q, k, v, score)
        up = jnp.concatenate([xf[i, every, :] for i in range(2)], axis=1) + dot((gate * o).astype(BF), wvo[...])
        up = up.astype(BF).astype(F32)
        for i in range(2):
            upf[i, every, :] = up[:, i * 128:(i + 1) * 128]
        both = dot_t(wlr[...], norm(up).astype(BF)) * row
        lf[pl.ds(b, HD, stride=8), :] = both[:HD]
        rf[pl.ds(pl.multiple_of(b * HD, HD), HD), :] = both[HD:]
        return carry

    lax.fori_loop(0, 8, col_one, 0)
    lsnd[...] = lf[...].astype(BF)
    rsnd[...] = rf[...].astype(BF)

    def lcopy(k):
        return copy(lsnd, lrcv.at[c], le_s.at[k], le_r.at[k], r, lax.rem(c + k, 16))

    for k in range(1, 16):
        lcopy(k).start()

    target = 2 * r + c // 8
    place = lax.rem(c, 8)
    self_row = jnp.where(target == c, r, -1)

    def rcopy(k, row):
        return copy(rsnd, rrcv.at[place], ri_s.at[k], ri_r.at[place], row, target)

    for k in range(8):
        @pl.when(self_row != k)
        def _():
            rcopy(k, k).start()

    @pl.when(target == c)
    def _():
        rrcv[place] = rsnd[...]

    for i in range(2):
        back_snd[:, :, i * 128:(i + 1) * 128] = upf[i].reshape(NC, 64, 128).astype(BF)

    def ucopy(k):
        to = lax.rem(c + k, 16)
        return copy(back_snd.at[to], back_rcv.at[c], u_s.at[k], u_r.at[k], r, to)

    for k in range(1, 16):
        ucopy(k).start()
    lrcv[c] = lsnd[...]
    back_rcv[c] = back_snd[c]

    for k in range(1, 16):
        lcopy(k).wait_recv()
    for i in range(HD):
        lt_out[i * R:(i + 1) * R, :] = jnp.concatenate(
            [lrcv[t, i * 8:(i + 1) * 8, :] for t in range(NC)], axis=0
        )

    source_row = blk
    for k in range(8):
        source_col = 8 * core + k

        @pl.when(jnp.logical_or(source_row != r, source_col != c))
        def _():
            copy(rsnd, rrcv.at[k], ri_s.at[k], ri_r.at[k], r, c).wait_recv()

    rt_out[...] = rrcv[...].reshape(8 * 256, 128)

    for k in range(1, 16):
        ucopy(k).wait_recv()
    for s in range(S):
        rows = [back_rcv[t, s * 8:(s + 1) * 8, :] for t in range(NC)]
        align[s] = jnp.concatenate(rows, axis=0)

    for g in range(G):
        for i in range(8):
            n_slot(g, i).wait_send()
        for k in range(1, 16):
            mcopy(g, k).wait_send()
    for k in range(1, 8):
        lv(k).wait_send()
    for k in range(1, 16):
        lc(k).wait_send()
        lcopy(k).wait_send()
        ucopy(k).wait_send()
    sib_copy.wait_send()
    for cp in b_slots + bc_slots:
        cp.wait_send()
    for k in range(8):
        @pl.when(self_row != k)
        def _():
            rcopy(k, k).wait_send()


def opm_kernel(lt, rt, inv, w, out, wt, acc):
    @pl.when(pl.program_id(0) == 0)
    def _():
        wt[...] = w[...].astype(F32).T.astype(BF)

    def step(t, carry):
        rows = rt[pl.ds(pl.multiple_of(t * 64, 64), 64), :]
        o = dot_t(rows, lt[...]).astype(BF)
        two = jnp.concatenate(
            [
                jnp.concatenate([o[j * HD:(j + 1) * HD, i * R:(i + 1) * R] for i in range(HD)], axis=0)
                for j in range(2)
            ],
            axis=1,
        )
        y = dot(wt[...], two)
        for j in range(2):
            one = y[:, j * R:(j + 1) * R] * inv[pl.ds(2 * t + j, 1), :]
            acc[pl.ds(2 * t + j, R, stride=16), :] = one.T
        return carry

    lax.fori_loop(0, 8, step, 0)
    out[...] = acc[...].reshape(R, 16, 128).astype(BF)


def per_device(fam, pair, present, valid, wh, wo, wb, wv, wvo, wlr, wz):
    vm = pl.BlockSpec(memory_space=pltpu.VMEM)
    dma = pltpu.SemaphoreType.DMA
    scratch = [
        pltpu.VMEM((NR, S, R, D), BF),
        pltpu.VMEM((NC, NR, S, R), F32),
        pltpu.VMEM((512, 128), F32),
        pltpu.VMEM((H, 64, 128), BF),
        pltpu.VMEM((H, 64, 128), BF),
        pltpu.VMEM((NR, H, R, 128), BF),
        pltpu.VMEM((S, R, D), BF),
        pltpu.VMEM((S, R, D), F32),
        pltpu.VMEM((NR * R, D), BF),
        pltpu.VMEM((NR * R, D), BF),
        pltpu.VMEM((2, R, D), F32),
        pltpu.VMEM((NC, 64, D), BF),
        pltpu.VMEM((NC, 64, D), BF),
        pltpu.VMEM((2, 1024, 128), F32),
        pltpu.VMEM((2, 1024, 128), F32),
        pltpu.VMEM((2, 1024, 128), F32),
        pltpu.VMEM((NC, 64, D), BF),
        pltpu.VMEM((NC, 64, D), BF),
        pltpu.VMEM((256, 128), F32),
        pltpu.VMEM((256, 128), F32),
        pltpu.VMEM((256, 128), BF),
        pltpu.VMEM((NC, 256, 128), BF),
        pltpu.VMEM((256, 128), BF),
        pltpu.VMEM((8, 256, 128), BF),
        pltpu.VMEM((R, 128), F32),
        pltpu.VMEM((R, 128), F32),
        dma((G, 8)), dma((G, 8)), dma((8,)), dma((8,)), dma((16,)), dma((16,)), dma, dma,
        dma((8,)), dma((8,)), dma((7,)), dma((7,)),
        dma((G, 16)), dma((G, 16)), dma((16,)), dma((16,)), dma((16,)), dma((16,)), dma((8,)), dma((8,)),
    ]
    align, lt, rt, inv = pl.pallas_call(
        msa_kernel,
        out_shape=(
            jax.ShapeDtypeStruct((S, R, D), BF),
            jax.ShapeDtypeStruct((HD * R, 128), BF),
            jax.ShapeDtypeStruct((2048, 128), BF),
            jax.ShapeDtypeStruct((64, 128), F32),
        ),
        in_specs=[vm] * 10,
        out_specs=(vm,) * 4,
        scratch_shapes=scratch,
        compiler_params=pltpu.CompilerParams(has_side_effects=True, vmem_limit_bytes=60 * 1024 * 1024),
        name="msa",
    )(
        fam, pair, present, valid.reshape(NR, R), wh, wo, wb.T, wv, wvo,
        wlr.transpose(0, 2, 1).reshape(64, D),
    )
    pair_out = pl.pallas_call(
        opm_kernel,
        grid=(4,),
        out_shape=jax.ShapeDtypeStruct((R, 64, 128), BF),
        in_specs=[
            pl.BlockSpec((HD * R, 128), lambda i: (0, 0)),
            pl.BlockSpec((512, 128), lambda i: (i, 0)),
            pl.BlockSpec((16, 128), lambda i: (i, 0)),
            pl.BlockSpec((1024, 128), lambda i: (0, 0)),
        ],
        out_specs=pl.BlockSpec((R, 16, 128), lambda i: (0, i, 0)),
        scratch_shapes=[pltpu.VMEM((128, 1024), BF), pltpu.VMEM((R * 16, 128), F32)],
        compiler_params=pltpu.CompilerParams(vmem_limit_bytes=40 * 1024 * 1024),
        name="opm",
    )(lt, rt, inv, wz)
    return align, pair_out


def solution(mesh):
    in_specs = (P("col", "row", None), P("row", "col", None), P("col", "row")) + (P(),) * 8
    out_specs = (P("col", "row", None), P("row", "col", None))
    return jax.shard_map(per_device, mesh=mesh, in_specs=in_specs, out_specs=out_specs, check_vma=False)
```

time: 453 us -> 156 us (0.34)
  Pallas kernels: 0 us -> 151 us
  matrix products: 122 us -> 0 us
  waiting for transfers between devices: 114 us -> 0 us
  blocking collectives: 82.6 us -> 0 us
  local copies, waits for them, and re-layouts: 60 us -> 3.82 us
  starting transfers between devices: 33.5 us -> 0 us
  other arithmetic: 24.6 us -> 0 us
  between operations: 14.2 us -> 0.67 us
    pallas_call x0 -> x2, Pallas kernels: none -> 151 us  [the longest x1 125 us: per_device(): pl.pallas_call(msa_kernel, out_shape=(jax.ShapeDtypeStruct((S, R, D), BF)...]
    dot_general x45 -> x0, matrix products: 117 us -> none  [the longest x8 43.4 us: row_one(): jnp.einsum('hij,jhd->ihd', weights, value_one.reshape(total_res, head_cou...]
    all_gather x3 -> x0, waiting for transfers between devices: 103 us -> none  [the longest x1 85.5 us: per_device(): lax.all_gather(standardized_source, 'row', axis=1, tiled=True)]
    all_gather x3 -> x0, blocking collectives: 67.7 us -> none  [the longest x1 24.7 us: per_device(): lax.all_gather(mask_three, 'col', axis=0, tiled=True)]
    all_to_all x4 -> x0, starting transfers between devices: 33.2 us -> none  [the longest x1 12 us: per_device(): lax.all_to_all(right_rows, 'col', split_axis=2, concat_axis=0, tiled=True)]
    while x34 -> x0, local copies, waits for them, and re-layouts: 21.5 us -> none
    dynamic_slice x41 -> x0, local copies, waits for them, and re-layouts: 15.2 us -> none  [the longest x40 14.4 us: per_device(): lax.map(row_one, (query_rows, key_rows, value_rows, mask_all))]
    all_to_all x1 -> x0, blocking collectives: 15 us -> none  [per_device(): lax.all_to_all(column_output, 'col', split_axis=0, concat_axis=1, tiled=T...]
  transfers between devices with their start and end apart: 7 -> 0, of which waited for: 3 -> 0; matrix products, arithmetic and copies ran while one was open for 29% -> 0% of each run, Pallas kernels for 0% -> 0%
where the time goes in v1:
time: 156 us
  Pallas kernels  151 us (97%)
  local copies, waits for them, and re-layouts  3.82 us (2%)
    pallas_call x1, Pallas kernels, per_device(): pl.pallas_call(msa_kernel, out_shape=(jax.ShapeDtypeStruct((S, R, D), BF)...  125 us
    pallas_call x1, Pallas kernels, per_device(): pl.pallas_call(opm_kernel, grid=(4,), out_shape=jax.ShapeDtypeStruct((R,...  26 us
    unnamed x11, local copies, waits for them, and re-layouts  3.82 us

profile of v1, /device:TPU:1, one launch (start us, length us, event | category | flops | bytes accessed | tf_op | source)
XLA Modules:
  0.0 155.9 jit_solution(6525138888241384908)
XLA Ops:
  0.6 0.0 copy-start.2
  0.6 125.4 %msa.1 = (bf16[8,128,256]{2,1,0:T(8,128)(2,1)}, bf16[4096,128]{1,0:T(8,128)(2,1)}, bf16[2048,128]{1,0:T(8,128)(2,1)}, f32[64,128]{1,0:T(8,128)}) custom-call(bf16[8,128,256]{2,1,0:T(8,128)(2,1)} %fam.1, bf16[128,64,128]{2,1,0:T(8,128)(2,1)} %pair.1, s32[8,128]{1,0:T(8,128)} %present.1, s32[8,128]{1,0:T(8,128)} %bitcast.6, bf16[4,256,256]{2,1,0:T(8,128)(2,1)} %wh.1, ...), custom_call_target="tpu_custom_call" | custom-call | tf_op jit(solution)/shard_map/msa/pallas_call | solution.py:454
  126.0 0.0 copy-done.2
  126.0 0.0 copy-start
  126.1 1.2 copy-done
  127.3 0.0 copy-start.1
  127.3 1.0 copy-done.1
  128.3 0.0 copy-start.3
  128.3 0.8 copy-done.3
  129.1 0.0 copy-start.4
  129.1 26.0 %opm.1 = bf16[128,64,128]{2,1,0:T(8,128)(2,1)} custom-call(bf16[4096,128]{1,0:T(8,128)(2,1)S(1)} %copy-done, bf16[2048,128]{1,0:T(8,128)(2,1)S(1)} %copy-done.1, f32[64,128]{1,0:T(8,128)S(1)} %copy-done.3, bf16[1024,128]{1,0:T(8,128)(2,1)S(1)} %copy-done.2), custom_call_target="tpu_custom_call" | custom-call | tf_op jit(solution)/shard_map/opm/pallas_call | solution.py:471
  155.1 0.0 copy-done.4
  155.1 0.8 copy.14
Async XLA Ops:
  0.6 125.4 %copy-start.2 = (bf16[1024,128]{1,0:T(8,128)(2,1)S(1)}, bf16[1024,128]{1,0:T(8,128)(2,1)}, u32[]{:S(2)}) copy-start(bf16[1024,128]{1,0:T(8,128)(2,1)} %w.1) | copy-start | bytes 786436
  126.0 1.2 copy-start
  127.3 1.0 copy-start.1
  128.3 0.8 copy-start.3
  129.1 26.0 %copy-start.4 = (bf16[8,128,256]{2,1,0:T(8,128)(2,1)S(1)}, bf16[8,128,256]{2,1,0:T(8,128)(2,1)}, u32[]{:S(2)}) copy-start(bf16[8,128,256]{2,1,0:T(8,128)(2,1)} %get-tuple-element.12) | copy-start | bytes 1572868

commit v2 on v1

v2 whole, which is shorter than its diff:
```python
import jax
import jax.numpy as jnp
from jax import lax
from jax.experimental import pallas as pl
from jax.experimental.pallas import tpu as pltpu
from jax.sharding import PartitionSpec as P

BF = jnp.bfloat16
F32 = jnp.float32
EPS = 1e-05
MASK_BIG = 1000000000.0
MESH = pl.DeviceIdType.MESH

NR = 8
NC = 16
S = 8
R = 128
D = 256
H = 8
HD = 32
G = 2
JT = 8


def norm(x):
    c = x - jnp.mean(x, axis=-1, keepdims=True)
    return c * lax.rsqrt(jnp.mean(c * c, axis=-1, keepdims=True) + EPS)


def dot(a, b):
    return jnp.dot(a, b, preferred_element_type=F32)


def dot_t(a, b):
    return lax.dot_general(a, b, (((1,), (1,)), ((), ())), preferred_element_type=F32)


def sigmoid(x):
    return 1.0 / (1.0 + jnp.exp(-x))


def head_lanes(rows):
    return lax.broadcasted_iota(jnp.int32, (rows, D), 1) // HD


def attend(q, k, v, score_of, step):
    n = q.shape[0]
    lanes = head_lanes(n)
    total = jnp.zeros((n, D), F32)
    for h0 in range(0, H, step):
        heads = range(h0, h0 + step)
        stacked = jnp.concatenate([jnp.where(lanes == h, q, jnp.zeros_like(q)) for h in heads], axis=0)
        raw = dot_t(stacked, k)
        parts, sums = [], []
        for at, h in enumerate(heads):
            s = score_of(h, raw[at * n:(at + 1) * n])
            p = jnp.exp(s - jnp.max(s, axis=-1, keepdims=True))
            sums.append(jnp.sum(p, axis=-1, keepdims=True))
            parts.append(p.astype(BF))
        out = dot(jnp.concatenate(parts, axis=0), v)
        for at, h in enumerate(heads):
            total = jnp.where(lanes == h, out[at * n:(at + 1) * n] * (1.0 / sums[at]), total)
    return total


def msa_kernel(
    fam, pair, present, valid, wh, wo, wb, wv, wvo, wlr, wz,
    align, pair_out,
    ft, nall, livr, lres, lcol, bscr, mine, sib, ball, qs, gs, ks, vs, midf, snd, rcv,
    xf, nf, upf, back_snd, back_rcv, lf, rf, lrcv, rsnd, rrcv, ltt, cmask, inv, ltall, wzt, acc, blocks,
    z_s, z_r, n_s, n_r, lv_s, lv_r, lr_s, lr_r, lc_s, lc_r, sb_s, sb_r, b_s, b_r, bc_s, bc_r,
    m_s, m_r, u_s, u_r, le_s, le_r, lw_s, lw_r, ri_s, ri_r, o_s,
):
    r = lax.axis_index("row")
    c = lax.axis_index("col")
    core = lax.rem(c, 2)
    blk = c // 2
    x, zl = r // 2, lax.rem(r, 2)
    y, zh = c // 4, lax.rem(blk, 2)
    z = zh * 2 + zl
    rz = 2 * x + 1 - zl
    cs = c + 1 - 2 * core
    target = 2 * r + c // 8
    self_row = jnp.where(target == c, r, -1)

    def wrap(i, n):
        return lax.rem(i + n, n)

    def copy(src, dst, ss, rs, row, col):
        return pltpu.make_async_remote_copy(
            src_ref=src, dst_ref=dst, send_sem=ss, recv_sem=rs, device_id=(row, col), device_id_type=MESH
        )

    barrier = pltpu.get_barrier_semaphore()

    def greet(row, col):
        pl.semaphore_signal(barrier, inc=1, device_id=(row, col), device_id_type=MESH)

    for k in range(1, NR):
        greet(wrap(r + k, NR), c)
    for k in range(1, NC):
        greet(r, wrap(c + k, NC))
        greet(rz, wrap(c + k, NC))
    for k in range(8):
        @pl.when(self_row != k)
        def _():
            greet(k, target)

        @pl.when(jnp.logical_or(blk != r, 8 * core + k != c))
        def _():
            greet(blk, 8 * core + k)

    z_copy = copy(fam.at[pl.ds(4 * (1 - zl), 4)], ft.at[zl], z_s, z_r, rz, c)

    xl, xr = wrap(x + 3, 4), wrap(x + 1, 4)
    n_plan = [
        (x, zl, 0, 2, xr), (x, zl, 0, 2, xl), (x, 1 - zl, 0, 2, xr), (x, 1 - zl, 0, 2, xl),
        (xl, zl, 0, 1, xr), (xr, zl, 1, 1, xl), (xl, 1 - zl, 0, 1, xr), (xr, 1 - zl, 1, 1, xl),
    ]

    def nc(g, i):
        xb, zb, lo, n, to = n_plan[i]
        ref = nall.at[xb, zb, pl.ds(2 * g + lo, n)]
        return copy(ref, ref, n_s.at[g, i], n_r.at[g, i], 2 * to + zl, c)

    first = core == 0
    h0 = core * 4

    def at(dp, dq):
        by = wrap(y + jnp.where(first, dq, dp), 4)
        bz = wrap(z + jnp.where(first, dp, dq), 4)
        return by, bz

    def bref(dp, dq, lo, n):
        by, bz = at(dp, dq)
        return ball.at[lax.rem(bz, 2), by * 2 + bz // 2, pl.ds(h0 + lo, n)]

    def bc(slot, dp, dq, lo, n, to_p, to_q):
        ty, tz = at(to_p, to_q)
        ref = bref(dp, dq, lo, n)
        return copy(ref, ref, b_s.at[slot], b_r.at[slot], 2 * x + lax.rem(tz, 2), 4 * ty + 2 * (tz // 2) + core)

    along = (0, 3, 1, 2)

    def b_slot(i):
        if i == 0:
            return bc(0, 0, 0, 0, 4, 1, 0)
        if i == 1:
            return bc(1, 0, 0, 0, 4, 3, 0)
        if i == 2:
            return bc(2, 3, 0, 0, 2, 1, 0)
        if i == 3:
            return bc(3, 1, 0, 2, 2, 3, 0)
        dp = along[(i - 4) % 4]
        if i < 8:
            return bc(i, dp, 0, 0, 4, 0, 1)
        if i < 12:
            return bc(i, dp, 0, 0, 4, 0, 3)
        if i < 16:
            return bc(i, dp, 3, 0, 2, 0, 1)
        return bc(i, dp, 1, 2, 2, 0, 3)

    def b_core(dp, dq):
        ref = bref(dp, dq, 0, 4)
        i = dp * 4 + dq - 1
        return copy(ref, ref, bc_s.at[i], bc_r.at[i], r, cs)

    def b_start(*slots):
        for i in slots:
            b_slot(i).start()

    def b_wait(*slots):
        for i in slots:
            b_slot(i).wait_recv()

    def b_swap(*pairs):
        for p in pairs:
            b_core(*p).start()

    livr[r] = (present[...] * valid[pl.ds(r, 1), :]).astype(F32)
    ft[zl] = fam[pl.ds(4 * zl, 4)]
    for s in range(4):
        nall[x, zl, s] = norm(ft[zl, s].astype(F32)).astype(BF)
    pl.semaphore_wait(barrier, jnp.where(target == c, 51, 53))
    z_copy.start()
    for i in (0, 1):
        for g in range(G):
            nc(g, i).start()

    def lv(k):
        return copy(livr.at[r], livr.at[r], lv_s.at[k], lv_r.at[k], wrap(r + k, NR), c)

    for k in range(1, NR):
        lv(k).start()

    def bias_step(t, carry):
        lo = pair[pl.ds(t * 8, 8)].astype(F32)
        hi = pair[pl.ds(64 + t * 8, 8)].astype(F32)
        rows = norm(jnp.concatenate([lo, hi], axis=1).reshape(1024, 128)).astype(BF)
        b = dot_t(wb[...], rows)
        for i in range(8):
            bscr[pl.ds(t * 64 + i * 8, 8), :] = b[:, i * 128:(i + 1) * 128]
        return carry

    lax.fori_loop(0, 8, bias_step, 0)
    for h in range(H):
        mine[h] = bscr[pl.ds(h, 64, stride=8), :].astype(BF)
    sib_copy = copy(mine, sib, sb_s, sb_r, r, cs)
    sib_copy.start()

    z_copy.wait_recv()
    for s in range(4):
        nall[x, 1 - zl, s] = norm(ft[1 - zl, s].astype(F32)).astype(BF)
    for i in (2, 3):
        for g in range(G):
            nc(g, i).start()

    sib_copy.wait_recv()
    low = lax.broadcasted_iota(jnp.int32, (64, 128), 1) < 64
    for h in range(H):
        a = mine[h].astype(F32)
        b = sib[h].astype(F32)
        left_part = jnp.where(first, a, b)
        right_part = jnp.where(first, b, a)
        ball[zl, blk, h, 0:64, :] = jnp.where(low, left_part, pltpu.roll(right_part, 64, 1)).astype(BF)
        ball[zl, blk, h, 64:128, :] = jnp.where(low, pltpu.roll(left_part, 64, 1), right_part).astype(BF)
    b_start(0, 1, 4, 8)
    for g in range(G):
        for i in (0, 1):
            nc(g, i).wait_recv()
        for i in (4, 5):
            nc(g, i).start()

    for zb in range(2):
        for s in range(4):
            rows = nall[x, zb, s]
            qs[s, zb * R:(zb + 1) * R, :] = (dot(rows, wh[0]) * (HD ** -0.5)).astype(BF)
            gs[s, zb * R:(zb + 1) * R, :] = sigmoid(dot(rows, wh[3]))

    b_wait(0, 1)
    b_start(2, 3, 5, 9, 6, 10)
    b_swap((3, 0), (1, 0))
    b_wait(4, 8)
    b_start(12, 16)
    b_swap((0, 3), (0, 1))
    for g in range(G):
        for i in (2, 3):
            nc(g, i).wait_recv()
        for i in (6, 7):
            nc(g, i).start()
    b_wait(2, 3)
    b_start(7, 11)
    b_swap((2, 0))

    for k in range(1, NR):
        lv(k).wait_recv()
    lres[c] = livr[r]
    lcol[c] = livr[blk]

    def lr(k):
        return copy(livr.at[r], lres.at[c], lr_s.at[k], lr_r.at[k], r, wrap(c + k, NC))

    def lc(k):
        to = wrap(c + k, NC)
        return copy(livr.at[to // 2], lcol.at[c], lc_s.at[k], lc_r.at[k], r, to)

    for k in range(1, NC):
        lr(k).start()
        lc(k).start()

    b_wait(5, 9)
    b_start(13, 17)
    b_swap((3, 3), (3, 1))
    b_wait(6, 10)
    b_start(14, 18)
    b_swap((1, 3), (1, 1))
    b_wait(12, 16)
    b_swap((0, 2))
    b_wait(7, 11)
    b_start(15, 19)
    b_swap((2, 3), (2, 1))
    b_wait(13, 17)
    b_swap((3, 2))
    b_wait(14, 18)
    b_swap((1, 2))
    b_wait(15, 19)
    b_swap((2, 2))
    for g in range(G):
        for i in (4, 5, 6, 7):
            nc(g, i).wait_recv()
    for i in range(1, 16):
        b_core(i // 4, i % 4).wait_recv()

    def mc(g, zb, k):
        to = wrap(c + k, NC)
        return copy(
            snd.at[zb, to, pl.ds(g * 16, 16)], rcv.at[c, zl, pl.ds(g * 16, 16)],
            m_s.at[g, jnp.where(zb == zl, 0, 1), k], m_r.at[g, jnp.where(zb == zl, 0, 1), k],
            2 * x + zb, to,
        )

    def group(g, carry):
        def row_one(i, carry):
            s = 2 * g + i
            for b in range(NR):
                rows = nall[b // 2, b % 2, s]
                ks[b * R:(b + 1) * R, :] = dot(rows, wh[1]).astype(BF)
                vs[b * R:(b + 1) * R, :] = dot(rows, wh[2]).astype(BF)
            keep = jnp.concatenate([livr[b, pl.ds(4 * zl + s, 1), :] for b in range(NR)], axis=1) > 0.5

            def score(h, raw):
                bias = jnp.concatenate(
                    [jnp.concatenate([ball[zb, b, h] for b in range(NR)], axis=1) for zb in range(2)], axis=0
                )
                return jnp.where(keep, raw + bias.astype(F32), -MASK_BIG)

            o = attend(qs[s], ks[...], vs[...], score, 1)
            delta = dot((gs[s] * o).astype(BF), wo[...])
            for zb in range(2):
                midf[i, zb] = ft[zb, s].astype(F32) + delta[zb * R:(zb + 1) * R]
            return carry

        lax.fori_loop(0, 2, row_one, 0)
        for zb in range(2):
            for t in range(NC):
                two = jnp.concatenate([midf[i, zb, t * 8:(t + 1) * 8, :] for i in range(2)], axis=0)
                snd[zb, t, pl.ds(pl.multiple_of(g * 16, 16), 16), :] = two.astype(BF)
        for k in range(NC):
            mc(g, 1 - zl, k).start()
            if k > 0:
                mc(g, zl, k).start()
        return carry

    lax.fori_loop(0, G, group, 0)
    rcv[c, zl] = snd[zl, c]

    for k in range(1, NC):
        lr(k).wait_recv()
        lc(k).wait_recv()
    by_res = lres[...].reshape(R, R).T
    cmask[...] = by_res
    ltt[...] = lcol[...].reshape(R, R).T
    right_live = ltt[pl.ds(pl.multiple_of(core * 64, 64), 64), :]
    inv[...] = 1.0 / jnp.maximum(dot_t(right_live.astype(BF), by_res.astype(BF)), 1.0)
    wzt[...] = wz[...].astype(F32).T.astype(BF)
    for g in range(G):
        for k in range(NC):
            mc(g, 1 - zl, k).wait_recv()
            if k > 0:
                mc(g, zl, k).wait_recv()

    def col_norm(t, carry):
        mid = rcv[t].reshape(64, D).astype(F32)
        rows = pl.ds(pl.multiple_of(t * 64, 64), 64)
        normed = norm(mid)
        for i in range(2):
            xf[i, rows, :] = mid[:, i * 128:(i + 1) * 128]
            nf[i, rows, :] = normed[:, i * 128:(i + 1) * 128]
        return carry

    lax.fori_loop(0, NC, col_norm, 0)

    def col_one(b, carry):
        every = pl.ds(b, R, stride=8)
        rows = jnp.concatenate([nf[i, every, :] for i in range(2)], axis=1).astype(BF)
        q = (dot(rows, wv[0]) * (HD ** -0.5)).astype(BF)
        k = dot(rows, wv[1]).astype(BF)
        v = dot(rows, wv[2]).astype(BF)
        gate = sigmoid(dot(rows, wv[3]))
        row = cmask[pl.ds(c * 8 + b, 1), :]

        def score(h, raw):
            return jnp.where(row > 0.5, raw, -MASK_BIG)

        o = attend(q, k, v, score, 2)
        up = jnp.concatenate([xf[i, every, :] for i in range(2)], axis=1) + dot((gate * o).astype(BF), wvo[...])
        up = up.astype(BF).astype(F32)
        for i in range(2):
            upf[i, every, :] = up[:, i * 128:(i + 1) * 128]
        both = dot_t(wlr[...], norm(up).astype(BF)) * row
        lf[pl.ds(b, HD, stride=8), :] = both[:HD]
        rf[pl.ds(pl.multiple_of(b * HD, HD), HD), :] = both[HD:]
        return carry

    lax.fori_loop(0, 8, col_one, 0)
    lrcv[c] = lf[...].astype(BF)
    rsnd[...] = rf[...].astype(BF)

    cz = c + 2 - 4 * zh
    cl, cr = wrap(c + 12, NC), wrap(c + 4, NC)

    def far(i):
        return i + 2 - 4 * lax.rem(i // 2, 2)

    l_plan = [
        (c, 0, 256, cz), (c, 0, 256, cr), (c, 0, 256, cl), (far(c), 0, 256, cr), (far(c), 0, 256, cl),
        (cl, 0, 128, cr), (cr, 128, 128, cl), (far(cl), 0, 128, cr), (far(cr), 128, 128, cl),
    ]

    def lslot(i):
        owner, lo, n, to = l_plan[i]
        ref = lrcv.at[owner, pl.ds(lo, n)]
        return copy(ref, ref, le_s.at[i], le_r.at[i], r, to)

    def lswap(i):
        ref = lrcv.at[wrap(c + 2 * i, NC)]
        return copy(ref, ref, lw_s.at[i], lw_r.at[i], r, cs)

    place = lax.rem(c, 8)

    def rcopy(k):
        return copy(rsnd, rrcv.at[place], ri_s.at[k], ri_r.at[place], k, target)

    for i in (0, 1, 2):
        lslot(i).start()
    lswap(0).start()
    for k in range(8):
        @pl.when(self_row != k)
        def _():
            rcopy(k).start()

    @pl.when(target == c)
    def _():
        rrcv[place] = rsnd[...]

    lslot(0).wait_recv()
    for i in (3, 4):
        lslot(i).start()
    for i in (1, 2):
        lslot(i).wait_recv()
    for i in (5, 6):
        lslot(i).start()
    for i in (2, 6):
        lswap(i).start()
    far_at = lax.rem(far(c) - c + NC, NC) // 2
    lswap(far_at).start()
    for i in (3, 4):
        lslot(i).wait_recv()
    for i in (7, 8):
        lslot(i).start()
    near = far_at
    lswap(lax.rem(near + 2, 8)).start()
    lswap(lax.rem(near + 6, 8)).start()
    for i in (5, 6):
        lslot(i).wait_recv()
    lswap(4).start()
    for i in (7, 8):
        lslot(i).wait_recv()
    lswap(lax.rem(near + 4, 8)).start()

    for i in range(2):
        back_snd[:, :, i * 128:(i + 1) * 128] = upf[i].reshape(NC, 64, 128).astype(BF)

    def uc(k):
        to = wrap(c + k, NC)
        return copy(back_snd.at[to], back_rcv.at[c], u_s.at[k], u_r.at[k], r, to)

    for k in range(1, NC):
        uc(k).start()
    back_rcv[c] = back_snd[c]

    for i in range(8):
        lswap(i).wait_recv()
    for i in range(HD):
        ltall[i * R:(i + 1) * R, :] = jnp.concatenate(
            [lrcv[t, i * 8:(i + 1) * 8, :] for t in range(NC)], axis=0
        )
    for k in range(8):
        @pl.when(jnp.logical_or(blk != r, 8 * core + k != c))
        def _():
            copy(rsnd, rrcv.at[k], ri_s.at[k], ri_r.at[k], r, c).wait_recv()

    def out_copy(q):
        return pltpu.make_async_copy(
            blocks.at[lax.rem(q, 2)], pair_out.at[:, pl.ds(pl.multiple_of(q * 16, 16), 16), :], o_s.at[lax.rem(q, 2)]
        )

    def sixteen(q, carry):
        def step(t, carry):
            rows = rrcv[2 * q + t]
            o = dot_t(rows, ltall[...]).astype(BF)
            for j0 in range(0, JT, 2):
                two = jnp.concatenate(
                    [
                        jnp.concatenate(
                            [o[j * HD:(j + 1) * HD, i * R:(i + 1) * R] for i in range(HD)], axis=0
                        )
                        for j in (j0, j0 + 1)
                    ],
                    axis=1,
                )
                prod = dot(wzt[...], two)
                for j in range(2):
                    place = t * JT + j0 + j
                    one = prod[:, j * R:(j + 1) * R] * inv[pl.ds(q * 16 + place, 1), :]
                    acc[pl.ds(place, R, stride=16), :] = one.T
            return carry

        lax.fori_loop(0, 2, step, 0)

        @pl.when(q >= 2)
        def _():
            out_copy(q - 2).wait()

        blocks[lax.rem(q, 2)] = acc[...].reshape(R, 16, 128).astype(BF)
        out_copy(q).start()
        return carry

    lax.fori_loop(0, 4, sixteen, 0)
    for k in range(1, NC):
        uc(k).wait_recv()
    for s in range(S):
        align[s] = jnp.concatenate([back_rcv[t, s * 8:(s + 1) * 8, :] for t in range(NC)], axis=0)
    out_copy(2).wait()
    out_copy(3).wait()

    z_copy.wait_send()
    sib_copy.wait_send()
    for g in range(G):
        for i in range(8):
            nc(g, i).wait_send()
        for k in range(NC):
            mc(g, 1 - zl, k).wait_send()
            if k > 0:
                mc(g, zl, k).wait_send()
    for k in range(1, NR):
        lv(k).wait_send()
    for k in range(1, NC):
        lr(k).wait_send()
        lc(k).wait_send()
        uc(k).wait_send()
    for i in range(20):
        b_slot(i).wait_send()
    for i in range(1, 16):
        b_core(i // 4, i % 4).wait_send()
    for i in range(9):
        lslot(i).wait_send()
    for i in range(8):
        lswap(i).wait_send()
    for k in range(8):
        @pl.when(self_row != k)
        def _():
            rcopy(k).wait_send()


def per_device(fam, pair, present, valid, wh, wo, wb, wv, wvo, wlr, wz):
    vm = pl.BlockSpec(memory_space=pltpu.VMEM)
    dma = pltpu.SemaphoreType.DMA

    def sems(*shape):
        return [dma(shape), dma(shape)]

    scratch = [
        pltpu.VMEM((2, 4, R, D), BF),
        pltpu.VMEM((4, 2, 4, R, D), BF),
        pltpu.VMEM((NR, S, R), F32),
        pltpu.VMEM((NC, S, R), F32),
        pltpu.VMEM((NC, S, R), F32),
        pltpu.VMEM((512, 128), F32),
        pltpu.VMEM((H, 64, 128), BF),
        pltpu.VMEM((H, 64, 128), BF),
        pltpu.VMEM((2, NR, H, R, 128), BF),
        pltpu.VMEM((4, 2 * R, D), BF),
        pltpu.VMEM((4, 2 * R, D), F32),
        pltpu.VMEM((NR * R, D), BF),
        pltpu.VMEM((NR * R, D), BF),
        pltpu.VMEM((2, 2, R, D), F32),
        pltpu.VMEM((2, NC, 32, D), BF),
        pltpu.VMEM((NC, 2, 32, D), BF),
        pltpu.VMEM((2, 1024, 128), F32),
        pltpu.VMEM((2, 1024, 128), F32),
        pltpu.VMEM((2, 1024, 128), F32),
        pltpu.VMEM((NC, 64, D), BF),
        pltpu.VMEM((NC, 64, D), BF),
        pltpu.VMEM((256, 128), F32),
        pltpu.VMEM((256, 128), F32),
        pltpu.VMEM((NC, 256, 128), BF),
        pltpu.VMEM((256, 128), BF),
        pltpu.VMEM((8, 256, 128), BF),
        pltpu.VMEM((R, 128), F32),
        pltpu.VMEM((R, 128), F32),
        pltpu.VMEM((64, 128), F32),
        pltpu.VMEM((HD * R, 128), BF),
        pltpu.VMEM((128, 1024), BF),
        pltpu.VMEM((R * 16, 128), F32),
        pltpu.VMEM((2, R, 16, 128), BF),
        dma, dma, *sems(G, 8), *sems(8), *sems(16), *sems(16), dma, dma, *sems(20), *sems(15),
        *sems(G, 2, 16), *sems(16), *sems(9), *sems(8), *sems(8), dma((2,)),
    ]
    return pl.pallas_call(
        msa_kernel,
        out_shape=(jax.ShapeDtypeStruct((S, R, D), BF), jax.ShapeDtypeStruct((R, 64, 128), BF)),
        in_specs=[vm] * 11,
        out_specs=(vm, pl.BlockSpec(memory_space=pl.ANY)),
        scratch_shapes=scratch,
        compiler_params=pltpu.CompilerParams(
            has_side_effects=True, collective_id=0, vmem_limit_bytes=60 * 1024 * 1024
        ),
        name="msa",
    )(
        fam, pair, present, valid.reshape(NR, R), wh, wo, wb.T, wv, wvo,
        wlr.transpose(0, 2, 1).reshape(64, D), wz,
    )


def solution(mesh):
    in_specs = (P("col", "row", None), P("row", "col", None), P("col", "row")) + (P(),) * 8
    out_specs = (P("col", "row", None), P("row", "col", None))
    return jax.shard_map(per_device, mesh=mesh, in_specs=in_specs, out_specs=out_specs, check_vma=False)
```

time: 156 us -> 111 us (0.71)
  Pallas kernels: 151 us -> 105 us
    pallas_call x1 -> x0, Pallas kernels: 26 us -> none  [per_device(): pl.pallas_call(opm_kernel, grid=(4,), out_shape=jax.ShapeDtypeStruct((R,...]
    pallas_call x1, Pallas kernels: 125 us -> 105 us  [per_device(): pl.pallas_call(msa_kernel, out_shape=(jax.ShapeDtypeStruct((S, R, D), BF)...]
    unnamed x11 -> x2, local copies, waits for them, and re-layouts: 3.82 us -> 4.95 us
where the time goes in v2:
time: 111 us; the launch traced here: 110 us
  Pallas kernels  105 us (95%)
  local copies, waits for them, and re-layouts  4.95 us (4%)
    pallas_call x1, Pallas kernels, per_device(): pl.pallas_call(msa_kernel, out_shape=(jax.ShapeDtypeStruct((S, R, D), BF)...  105 us
    unnamed x2, local copies, waits for them, and re-layouts  4.95 us

profile of v2, /device:TPU:1, one launch (start us, length us, event | category | flops | bytes accessed | tf_op | source)
XLA Modules:
  0.0 110.1 jit_solution(15354084210040681976)
XLA Ops:
  0.6 104.5 %msa.1 = (bf16[8,128,256]{2,1,0:T(8,128)(2,1)}, bf16[128,64,128]{2,1,0:T(8,128)(2,1)}) custom-call(bf16[8,128,256]{2,1,0:T(8,128)(2,1)} %fam.1, bf16[128,64,128]{2,1,0:T(8,128)(2,1)} %pair.1, s32[8,128]{1,0:T(8,128)} %present.1, s32[8,128]{1,0:T(8,128)} %bitcast.6, bf16[4,256,256]{2,1,0:T(8,128)(2,1)} %wh.1, bf16[256,256]{1,0:T(8,128)(2,1)} %wo.1, ...), custom_call_target="tpu_custom_call" | custom-call | tf_op jit(solution)/shard_map/msa/pallas_call | solution.py:590
  105.2 1.9 %copy.15 = bf16[8,128,256]{2,1,0:T(8,128)(2,1)} copy(bf16[8,128,256]{2,1,0:T(8,128)(2,1)} %get-tuple-element.4) | data formatting | bytes 1048576
  107.1 3.1 %copy.16 = bf16[128,64,128]{2,1,0:T(8,128)(2,1)} copy(bf16[128,64,128]{2,1,0:T(8,128)(2,1)} %get-tuple-element.5) | data formatting | bytes 4194304

commit v3 on v2

--- a/solution.py
+++ b/solution.py
@@ -19,7 +19,7 @@
 H = 8
 HD = 32
 G = 2
-JT = 8
+NB = 4
 
 
 def norm(x):
@@ -66,7 +66,7 @@
 def msa_kernel(
     fam, pair, present, valid, wh, wo, wb, wv, wvo, wlr, wz,
     align, pair_out,
-    ft, nall, livr, lres, lcol, bscr, mine, sib, ball, qs, gs, ks, vs, midf, snd, rcv,
+    ft, nall, livr, lres, lcol, bscr, mine, sib, ball, qs, gs, ks, vs, midf, cqs, cks, cvs, cgs, cos, snd, rcv,
     xf, nf, upf, back_snd, back_rcv, lf, rf, lrcv, rsnd, rrcv, ltt, cmask, inv, ltall, wzt, acc, blocks,
     z_s, z_r, n_s, n_r, lv_s, lv_r, lr_s, lr_r, lc_s, lc_r, sb_s, sb_r, b_s, b_r, bc_s, bc_r,
     m_s, m_r, u_s, u_r, le_s, le_r, lw_s, lw_r, ri_s, ri_r, o_s,
@@ -110,7 +110,9 @@
         def _():
             greet(blk, 8 * core + k)
 
-    z_copy = copy(fam.at[pl.ds(4 * (1 - zl), 4)], ft.at[zl], z_s, z_r, rz, c)
+    def zc(g):
+        src = fam.at[pl.ds(4 * (1 - zl) + 2 * g, 2)]
+        return copy(src, ft.at[zl, pl.ds(2 * g, 2)], z_s.at[g], z_r.at[g], rz, c)
 
     xl, xr = wrap(x + 3, 4), wrap(x + 1, 4)
     n_plan = [
@@ -182,9 +184,9 @@
     for s in range(4):
         nall[x, zl, s] = norm(ft[zl, s].astype(F32)).astype(BF)
     pl.semaphore_wait(barrier, jnp.where(target == c, 51, 53))
-    z_copy.start()
-    for i in (0, 1):
-        for g in range(G):
+    for g in range(G):
+        zc(g).start()
+        for i in (0, 1):
             nc(g, i).start()
 
     def lv(k):
@@ -208,11 +210,11 @@
     sib_copy = copy(mine, sib, sb_s, sb_r, r, cs)
     sib_copy.start()
 
-    z_copy.wait_recv()
-    for s in range(4):
-        nall[x, 1 - zl, s] = norm(ft[1 - zl, s].astype(F32)).astype(BF)
-    for i in (2, 3):
-        for g in range(G):
+    for g in range(G):
+        zc(g).wait_recv()
+        for s in (2 * g, 2 * g + 1):
+            nall[x, 1 - zl, s] = norm(ft[1 - zl, s].astype(F32)).astype(BF)
+        for i in (2, 3):
             nc(g, i).start()
 
     sib_copy.wait_recv()
@@ -225,11 +227,14 @@
         ball[zl, blk, h, 0:64, :] = jnp.where(low, left_part, pltpu.roll(right_part, 64, 1)).astype(BF)
         ball[zl, blk, h, 64:128, :] = jnp.where(low, pltpu.roll(left_part, 64, 1), right_part).astype(BF)
     b_start(0, 1, 4, 8)
-    for g in range(G):
-        for i in (0, 1):
-            nc(g, i).wait_recv()
-        for i in (4, 5):
-            nc(g, i).start()
+
+    def pass_on(g, i):
+        for k in (i, i + 1):
+            nc(g, k).wait_recv()
+        for k in (i + 4, i + 5):
+            nc(g, k).start()
+
+    pass_on(0, 0)
 
     for zb in range(2):
         for s in range(4):
@@ -240,17 +245,15 @@
     b_wait(0, 1)
     b_start(2, 3, 5, 9, 6, 10)
     b_swap((3, 0), (1, 0))
+    pass_on(0, 2)
     b_wait(4, 8)
     b_start(12, 16)
     b_swap((0, 3), (0, 1))
-    for g in range(G):
-        for i in (2, 3):
-            nc(g, i).wait_recv()
-        for i in (6, 7):
-            nc(g, i).start()
+    pass_on(1, 0)
     b_wait(2, 3)
     b_start(7, 11)
     b_swap((2, 0))
+    pass_on(1, 2)
 
     for k in range(1, NR):
         lv(k).wait_recv()
@@ -285,9 +288,17 @@
     b_swap((1, 2))
     b_wait(15, 19)
     b_swap((2, 2))
-    for g in range(G):
+
+    def keys_values(g):
         for i in (4, 5, 6, 7):
             nc(g, i).wait_recv()
+        for s in (2 * g, 2 * g + 1):
+            for b in range(NR):
+                rows = nall[b // 2, b % 2, s]
+                ks[s, b * R:(b + 1) * R, :] = dot(rows, wh[1]).astype(BF)
+                vs[s, b * R:(b + 1) * R, :] = dot(rows, wh[2]).astype(BF)
+
+    keys_values(0)
     for i in range(1, 16):
         b_core(i // 4, i % 4).wait_recv()
 
@@ -299,13 +310,9 @@
             2 * x + zb, to,
         )
 
-    def group(g, carry):
+    def group(g):
         def row_one(i, carry):
             s = 2 * g + i
-            for b in range(NR):
-                rows = nall[b // 2, b % 2, s]
-                ks[b * R:(b + 1) * R, :] = dot(rows, wh[1]).astype(BF)
-                vs[b * R:(b + 1) * R, :] = dot(rows, wh[2]).astype(BF)
             keep = jnp.concatenate([livr[b, pl.ds(4 * zl + s, 1), :] for b in range(NR)], axis=1) > 0.5
 
             def score(h, raw):
@@ -314,7 +321,7 @@
                 )
                 return jnp.where(keep, raw + bias.astype(F32), -MASK_BIG)
 
-            o = attend(qs[s], ks[...], vs[...], score, 1)
+            o = attend(qs[s], ks[s], vs[s], score, 1)
             delta = dot((gs[s] * o).astype(BF), wo[...])
             for zb in range(2):
                 midf[i, zb] = ft[zb, s].astype(F32) + delta[zb * R:(zb + 1) * R]
@@ -324,14 +331,15 @@
         for zb in range(2):
             for t in range(NC):
                 two = jnp.concatenate([midf[i, zb, t * 8:(t + 1) * 8, :] for i in range(2)], axis=0)
-                snd[zb, t, pl.ds(pl.multiple_of(g * 16, 16), 16), :] = two.astype(BF)
+                snd[zb, t, g * 16:(g + 1) * 16, :] = two.astype(BF)
         for k in range(NC):
             mc(g, 1 - zl, k).start()
             if k > 0:
                 mc(g, zl, k).start()
-        return carry
-
-    lax.fori_loop(0, G, group, 0)
+
+    group(0)
+    keys_values(1)
+    group(1)
     rcv[c, zl] = snd[zl, c]
 
     for k in range(1, NC):
@@ -360,31 +368,41 @@
 
     lax.fori_loop(0, NC, col_norm, 0)
 
-    def col_one(b, carry):
-        every = pl.ds(b, R, stride=8)
-        rows = jnp.concatenate([nf[i, every, :] for i in range(2)], axis=1).astype(BF)
-        q = (dot(rows, wv[0]) * (HD ** -0.5)).astype(BF)
-        k = dot(rows, wv[1]).astype(BF)
-        v = dot(rows, wv[2]).astype(BF)
-        gate = sigmoid(dot(rows, wv[3]))
-        row = cmask[pl.ds(c * 8 + b, 1), :]
-
-        def score(h, raw):
-            return jnp.where(row > 0.5, raw, -MASK_BIG)
-
-        o = attend(q, k, v, score, 2)
-        up = jnp.concatenate([xf[i, every, :] for i in range(2)], axis=1) + dot((gate * o).astype(BF), wvo[...])
-        up = up.astype(BF).astype(F32)
-        for i in range(2):
-            upf[i, every, :] = up[:, i * 128:(i + 1) * 128]
-        both = dot_t(wlr[...], norm(up).astype(BF)) * row
-        lf[pl.ds(b, HD, stride=8), :] = both[:HD]
-        rf[pl.ds(pl.multiple_of(b * HD, HD), HD), :] = both[HD:]
-        return carry
-
-    lax.fori_loop(0, 8, col_one, 0)
-    lrcv[c] = lf[...].astype(BF)
-    rsnd[...] = rf[...].astype(BF)
+    def rows_of(ref, p):
+        return jnp.concatenate(
+            [
+                jnp.concatenate([ref[i, pl.ds(p * NB + b, R, stride=8), :] for i in range(2)], axis=1)
+                for b in range(NB)
+            ],
+            axis=0,
+        )
+
+    def col_half(p):
+        rows = rows_of(nf, p).astype(BF)
+        cqs[...] = (dot(rows, wv[0]) * (HD ** -0.5)).astype(BF)
+        cks[...] = dot(rows, wv[1]).astype(BF)
+        cvs[...] = dot(rows, wv[2]).astype(BF)
+        cgs[...] = sigmoid(dot(rows, wv[3]))
+        for b in range(NB):
+            row = cmask[pl.ds(c * 8 + p * NB + b, 1), :]
+            span = slice(b * R, (b + 1) * R)
+
+            def score(h, raw):
+                return jnp.where(row > 0.5, raw, -MASK_BIG)
+
+            o = attend(cqs[span, :], cks[span, :], cvs[span, :], score, 2)
+            cos[span, :] = (cgs[span, :] * o).astype(BF)
+        up = (rows_of(xf, p) + dot(cos[...], wvo[...])).astype(BF).astype(F32)
+        both = dot_t(wlr[...], norm(up).astype(BF))
+        for b in range(NB):
+            span = slice(b * R, (b + 1) * R)
+            for i in range(2):
+                upf[i, pl.ds(p * NB + b, R, stride=8), :] = up[span, i * 128:(i + 1) * 128]
+            one = both[:, span] * cmask[pl.ds(c * 8 + p * NB + b, 1), :]
+            lf[pl.ds(p * 128 + b, HD, stride=NB), :] = one[:HD]
+            rf[(p * NB + b) * HD:(p * NB + b + 1) * HD, :] = one[HD:]
+        lrcv[c, p * 128:(p + 1) * 128, :] = lf[p * 128:(p + 1) * 128, :].astype(BF)
+        rsnd[p * 128:(p + 1) * 128, :] = rf[p * 128:(p + 1) * 128, :].astype(BF)
 
     cz = c + 2 - 4 * zh
     cl, cr = wrap(c + 12, NC), wrap(c + 4, NC)
@@ -393,60 +411,86 @@
         return i + 2 - 4 * lax.rem(i // 2, 2)
 
     l_plan = [
-        (c, 0, 256, cz), (c, 0, 256, cr), (c, 0, 256, cl), (far(c), 0, 256, cr), (far(c), 0, 256, cl),
-        (cl, 0, 128, cr), (cr, 128, 128, cl), (far(cl), 0, 128, cr), (far(cr), 128, 128, cl),
+        (c, 0, 128, cz), (c, 0, 128, cr), (c, 0, 128, cl), (far(c), 0, 128, cr), (far(c), 0, 128, cl),
+        (cl, 0, 64, cr), (cr, 64, 64, cl), (far(cl), 0, 64, cr), (far(cr), 64, 64, cl),
     ]
-
-    def lslot(i):
+    near = lax.rem(far(c) - c + NC, NC) // 2
+
+    def lslot(p, i):
         owner, lo, n, to = l_plan[i]
-        ref = lrcv.at[owner, pl.ds(lo, n)]
-        return copy(ref, ref, le_s.at[i], le_r.at[i], r, to)
-
-    def lswap(i):
-        ref = lrcv.at[wrap(c + 2 * i, NC)]
-        return copy(ref, ref, lw_s.at[i], lw_r.at[i], r, cs)
+        ref = lrcv.at[owner, pl.ds(p * 128 + lo, n)]
+        return copy(ref, ref, le_s.at[p, i], le_r.at[p, i], r, to)
+
+    def lswap(p, i):
+        ref = lrcv.at[wrap(c + 2 * i, NC), pl.ds(p * 128, 128)]
+        return copy(ref, ref, lw_s.at[p, i], lw_r.at[p, i], r, cs)
 
     place = lax.rem(c, 8)
 
-    def rcopy(k):
-        return copy(rsnd, rrcv.at[place], ri_s.at[k], ri_r.at[place], k, target)
-
-    for i in (0, 1, 2):
-        lslot(i).start()
-    lswap(0).start()
-    for k in range(8):
-        @pl.when(self_row != k)
-        def _():
-            rcopy(k).start()
+    def rcopy(p, k):
+        span = pl.ds(p * 128, 128)
+        return copy(rsnd.at[span], rrcv.at[place, span], ri_s.at[p, k], ri_r.at[p, place], k, target)
+
+    def left_one(p):
+        for i in (0, 1, 2):
+            lslot(p, i).start()
+        lswap(p, 0).start()
+
+    def left_two(p):
+        for i in (0, 1, 2):
+            lslot(p, i).wait_recv()
+        for i in (3, 4, 5, 6):
+            lslot(p, i).start()
+        lswap(p, near).start()
+        lswap(p, 2).start()
+        lswap(p, 6).start()
+
+    def left_three(p):
+        for i in (3, 4):
+            lslot(p, i).wait_recv()
+        for i in (7, 8):
+            lslot(p, i).start()
+        lswap(p, lax.rem(near + 2, 8)).start()
+        lswap(p, lax.rem(near + 6, 8)).start()
+        for i in (5, 6):
+            lslot(p, i).wait_recv()
+        lswap(p, 4).start()
+
+    def left_four(p):
+        for i in (7, 8):
+            lslot(p, i).wait_recv()
+        lswap(p, lax.rem(near + 4, 8)).start()
+
+    def right_send(p):
+        for k in range(8):
+            @pl.when(self_row != k)
+            def _():
+                rcopy(p, k).start()
+
+    def right_wait(p):
+        span = pl.ds(p * 128, 128)
+        for k in range(8):
+            @pl.when(jnp.logical_or(blk != r, 8 * core + k != c))
+            def _():
+                copy(rsnd.at[span], rrcv.at[k, span], ri_s.at[p, k], ri_r.at[p, k], r, c).wait_recv()
+
+    col_half(0)
+    left_one(0)
+    right_send(0)
+    col_half(1)
+    left_one(1)
+    left_two(0)
+    left_two(1)
+    left_three(0)
+    left_three(1)
+    right_send(1)
 
     @pl.when(target == c)
     def _():
         rrcv[place] = rsnd[...]
 
-    lslot(0).wait_recv()
-    for i in (3, 4):
-        lslot(i).start()
-    for i in (1, 2):
-        lslot(i).wait_recv()
-    for i in (5, 6):
-        lslot(i).start()
-    for i in (2, 6):
-        lswap(i).start()
-    far_at = lax.rem(far(c) - c + NC, NC) // 2
-    lswap(far_at).start()
-    for i in (3, 4):
-        lslot(i).wait_recv()
-    for i in (7, 8):
-        lslot(i).start()
-    near = far_at
-    lswap(lax.rem(near + 2, 8)).start()
-    lswap(lax.rem(near + 6, 8)).start()
-    for i in (5, 6):
-        lslot(i).wait_recv()
-    lswap(4).start()
-    for i in (7, 8):
-        lslot(i).wait_recv()
-    lswap(lax.rem(near + 4, 8)).start()
+    left_four(0)
+    left_four(1)
 
     for i in range(2):
         back_snd[:, :, i * 128:(i + 1) * 128] = upf[i].reshape(NC, 64, 128).astype(BF)
@@ -459,54 +503,60 @@
         uc(k).start()
     back_rcv[c] = back_snd[c]
 
-    for i in range(8):
-        lswap(i).wait_recv()
-    for i in range(HD):
-        ltall[i * R:(i + 1) * R, :] = jnp.concatenate(
-            [lrcv[t, i * 8:(i + 1) * 8, :] for t in range(NC)], axis=0
-        )
-    for k in range(8):
-        @pl.when(jnp.logical_or(blk != r, 8 * core + k != c))
-        def _():
-            copy(rsnd, rrcv.at[k], ri_s.at[k], ri_r.at[k], r, c).wait_recv()
+    for p in range(2):
+        for i in range(8):
+            lswap(p, i).wait_recv()
+    low4 = lax.rem(lax.broadcasted_iota(jnp.int32, (R, 128), 0), 8) < 4
+    for m in range(16):
+        a = lrcv[:, m * 8:(m + 1) * 8, :].astype(F32).reshape(R, 128)
+        b = lrcv[:, 128 + m * 8:128 + (m + 1) * 8, :].astype(F32).reshape(R, 128)
+        ltall[2 * m * R:(2 * m + 1) * R, :] = jnp.where(low4, a, pltpu.roll(b, 4, 0)).astype(BF)
+        ltall[(2 * m + 1) * R:(2 * m + 2) * R, :] = jnp.where(low4, pltpu.roll(a, R - 4, 0), b).astype(BF)
 
     def out_copy(q):
         return pltpu.make_async_copy(
             blocks.at[lax.rem(q, 2)], pair_out.at[:, pl.ds(pl.multiple_of(q * 16, 16), 16), :], o_s.at[lax.rem(q, 2)]
         )
 
-    def sixteen(q, carry):
-        def step(t, carry):
-            rows = rrcv[2 * q + t]
-            o = dot_t(rows, ltall[...]).astype(BF)
-            for j0 in range(0, JT, 2):
-                two = jnp.concatenate(
-                    [
-                        jnp.concatenate(
-                            [o[j * HD:(j + 1) * HD, i * R:(i + 1) * R] for i in range(HD)], axis=0
-                        )
-                        for j in (j0, j0 + 1)
-                    ],
-                    axis=1,
-                )
-                prod = dot(wzt[...], two)
-                for j in range(2):
-                    place = t * JT + j0 + j
-                    one = prod[:, j * R:(j + 1) * R] * inv[pl.ds(q * 16 + place, 1), :]
-                    acc[pl.ds(place, R, stride=16), :] = one.T
-            return carry
-
-        lax.fori_loop(0, 2, step, 0)
+    def eight(q, p):
+        rows = jnp.concatenate([rrcv[2 * q + t, p * 128:(p + 1) * 128, :] for t in range(2)], axis=0)
+        o = dot_t(rows, ltall[...]).astype(BF)
+        for j0 in range(0, 8, 2):
+            two = jnp.concatenate(
+                [
+                    jnp.concatenate([o[j * HD:(j + 1) * HD, i * R:(i + 1) * R] for i in range(HD)], axis=0)
+                    for j in (j0, j0 + 1)
+                ],
+                axis=1,
+            )
+            prod = dot(wzt[...], two)
+            for i in range(2):
+                j = q * 16 + (j0 + i) // NB * 8 + p * NB + (j0 + i) % NB
+                one = prod[:, i * R:(i + 1) * R] * inv[pl.ds(j, 1), :]
+                acc[pl.ds(j, R, stride=64), :] = one.T
+
+    def first_half(q, carry):
+        eight(q, 0)
+        return carry
+
+    def second_half(q, carry):
+        eight(q, 1)
 
         @pl.when(q >= 2)
         def _():
             out_copy(q - 2).wait()
 
-        blocks[lax.rem(q, 2)] = acc[...].reshape(R, 16, 128).astype(BF)
+        for t in range(4):
+            @pl.when(q == t)
+            def _():
+                blocks[t % 2] = acc[...].reshape(R, 64, 128)[:, t * 16:(t + 1) * 16, :].astype(BF)
         out_copy(q).start()
         return carry
 
-    lax.fori_loop(0, 4, sixteen, 0)
+    right_wait(0)
+    lax.fori_loop(0, 4, first_half, 0)
+    right_wait(1)
+    lax.fori_loop(0, 4, second_half, 0)
     for k in range(1, NC):
         uc(k).wait_recv()
     for s in range(S):
@@ -514,7 +564,8 @@
     out_copy(2).wait()
     out_copy(3).wait()
 
-    z_copy.wait_send()
+    for g in range(G):
+        zc(g).wait_send()
     sib_copy.wait_send()
     for g in range(G):
         for i in range(8):
@@ -533,14 +584,26 @@
         b_slot(i).wait_send()
     for i in range(1, 16):
         b_core(i // 4, i % 4).wait_send()
-    for i in range(9):
-        lslot(i).wait_send()
-    for i in range(8):
-        lswap(i).wait_send()
-    for k in range(8):
-        @pl.when(self_row != k)
-        def _():
-            rcopy(k).wait_send()
+    for p in range(2):
+        for i in range(9):
+            lslot(p, i).wait_send()
+        for i in range(8):
+            lswap(p, i).wait_send()
+        for k in range(8):
+            @pl.when(self_row != k)
+            def _():
+                rcopy(p, k).wait_send()
+
+
+def relay_kernel(a, b, a_out, b_out, sem):
+    copies = [pltpu.make_async_copy(a, a_out, sem.at[0])]
+    for i in range(4):
+        rows = pl.ds(i * 32, 32)
+        copies.append(pltpu.make_async_copy(b.at[rows], b_out.at[rows], sem.at[1 + i]))
+    for cp in copies:
+        cp.start()
+    for cp in copies:
+        cp.wait()
 
 
 def per_device(fam, pair, present, valid, wh, wo, wb, wv, wvo, wlr, wz):
@@ -562,9 +625,14 @@
         pltpu.VMEM((2, NR, H, R, 128), BF),
         pltpu.VMEM((4, 2 * R, D), BF),
         pltpu.VMEM((4, 2 * R, D), F32),
-        pltpu.VMEM((NR * R, D), BF),
-        pltpu.VMEM((NR * R, D), BF),
+        pltpu.VMEM((4, NR * R, D), BF),
+        pltpu.VMEM((4, NR * R, D), BF),
         pltpu.VMEM((2, 2, R, D), F32),
+        pltpu.VMEM((NB * R, D), BF),
+        pltpu.VMEM((NB * R, D), BF),
+        pltpu.VMEM((NB * R, D), BF),
+        pltpu.VMEM((NB * R, D), F32),
+        pltpu.VMEM((NB * R, D), BF),
         pltpu.VMEM((2, NC, 32, D), BF),
         pltpu.VMEM((NC, 2, 32, D), BF),
         pltpu.VMEM((2, 1024, 128), F32),
@@ -582,12 +650,12 @@
         pltpu.VMEM((64, 128), F32),
         pltpu.VMEM((HD * R, 128), BF),
         pltpu.VMEM((128, 1024), BF),
-        pltpu.VMEM((R * 16, 128), F32),
+        pltpu.VMEM((R * 64, 128), F32),
         pltpu.VMEM((2, R, 16, 128), BF),
-        dma, dma, *sems(G, 8), *sems(8), *sems(16), *sems(16), dma, dma, *sems(20), *sems(15),
-        *sems(G, 2, 16), *sems(16), *sems(9), *sems(8), *sems(8), dma((2,)),
+        *sems(G), *sems(G, 8), *sems(8), *sems(16), *sems(16), dma, dma, *sems(20), *sems(15),
+        *sems(G, 2, 16), *sems(16), *sems(2, 9), *sems(2, 8), *sems(2, 8), dma((2,)),
     ]
-    return pl.pallas_call(
+    align, pair_out = pl.pallas_call(
         msa_kernel,
         out_shape=(jax.ShapeDtypeStruct((S, R, D), BF), jax.ShapeDtypeStruct((R, 64, 128), BF)),
         in_specs=[vm] * 11,
@@ -601,6 +669,16 @@
         fam, pair, present, valid.reshape(NR, R), wh, wo, wb.T, wv, wvo,
         wlr.transpose(0, 2, 1).reshape(64, D), wz,
     )
+    anywhere = pl.BlockSpec(memory_space=pl.ANY)
+    return pl.pallas_call(
+        relay_kernel,
+        out_shape=(jax.ShapeDtypeStruct((S, R, D), BF), jax.ShapeDtypeStruct((R, 64, 128), BF)),
+        in_specs=[anywhere] * 2,
+        out_specs=(anywhere,) * 2,
+        scratch_shapes=[dma((5,))],
+        compiler_params=pltpu.CompilerParams(vmem_limit_bytes=60 * 1024 * 1024),
+        name="relay",
+    )(align, pair_out)
 
 
 def solution(mesh):

time: 111 us -> 181 us (1.63)
  Pallas kernels: 105 us -> 179 us
  local copies, waits for them, and re-layouts: 4.95 us -> 0 us
    pallas_call x0 -> x1, Pallas kernels: none -> 80.6 us  [per_device(): pl.pallas_call(relay_kernel, out_shape=(jax.ShapeDtypeStruct((S, R, D), B...]
    pallas_call x1, Pallas kernels: 105 us -> 98.9 us  [per_device(): pl.pallas_call(msa_kernel, out_shape=(jax.ShapeDtypeStruct((S, R, D), BF)...]
    unnamed x2 -> x0, local copies, waits for them, and re-layouts: 4.95 us -> none
where the time goes in v3:
time: 181 us; the launch traced here: 180 us
  Pallas kernels  179 us (99%)
    pallas_call x1, Pallas kernels, per_device(): pl.pallas_call(msa_kernel, out_shape=(jax.ShapeDtypeStruct((S, R, D), BF)...  98.9 us
    pallas_call x1, Pallas kernels, per_device(): pl.pallas_call(relay_kernel, out_shape=(jax.ShapeDtypeStruct((S, R, D), B...  80.6 us

profile of v3, /device:TPU:1, one launch (start us, length us, event | category | flops | bytes accessed | tf_op | source)
XLA Modules:
  0.0 180.2 jit_solution(7485655355439833428)
XLA Ops:
  0.6 98.9 %msa.1 = (bf16[8,128,256]{2,1,0:T(8,128)(2,1)}, bf16[128,64,128]{2,1,0:T(8,128)(2,1)}) custom-call(bf16[8,128,256]{2,1,0:T(8,128)(2,1)} %fam.1, bf16[128,64,128]{2,1,0:T(8,128)(2,1)} %pair.1, s32[8,128]{1,0:T(8,128)} %present.1, s32[8,128]{1,0:T(8,128)} %bitcast.6, bf16[4,256,256]{2,1,0:T(8,128)(2,1)} %wh.1, bf16[256,256]{1,0:T(8,128)(2,1)} %wo.1, ...), custom_call_target="tpu_custom_call" | custom-call | tf_op jit(solution)/shard_map/msa/pallas_call | solution.py:658
  99.5 80.6 %relay.1 = (bf16[8,128,256]{2,1,0:T(8,128)(2,1)}, bf16[128,64,128]{2,1,0:T(8,128)(2,1)}) custom-call(bf16[8,128,256]{2,1,0:T(8,128)(2,1)} %get-tuple-element.4.a, bf16[128,64,128]{2,1,0:T(8,128)(2,1)} %get-tuple-element.5.b), custom_call_target="tpu_custom_call" | custom-call | tf_op jit(solution)/shard_map/relay/pallas_call | solution.py:673

commit v4 on v3

--- a/solution.py
+++ b/solution.py
@@ -64,12 +64,12 @@
 
 
 def msa_kernel(
-    fam, pair, present, valid, wh, wo, wb, wv, wvo, wlr, wz,
+    fam_in, pair_in, present, valid, wh_in, wo_in, wb, wv_in, wvo_in, wlr, wz_in,
     align, pair_out,
-    ft, nall, livr, lres, lcol, bscr, mine, sib, ball, qs, gs, ks, vs, midf, cqs, cks, cvs, cgs, cos, snd, rcv,
+    fam, pair, wh, wo, wv, wvo, wz, ft, nall, livr, lres, lcol, bscr, mine, sib, ball, qs, gs, ks, vs, midf, cqs, cks, cvs, cgs, cos, snd, rcv,
     xf, nf, upf, back_snd, back_rcv, lf, rf, lrcv, rsnd, rrcv, ltt, cmask, inv, ltall, wzt, acc, blocks,
     z_s, z_r, n_s, n_r, lv_s, lv_r, lr_s, lr_r, lc_s, lc_r, sb_s, sb_r, b_s, b_r, bc_s, bc_r,
-    m_s, m_r, u_s, u_r, le_s, le_r, lw_s, lw_r, ri_s, ri_r, o_s,
+    m_s, m_r, u_s, u_r, le_s, le_r, lw_s, lw_r, ri_s, ri_r, o_s, in_s,
 ):
     r = lax.axis_index("row")
     c = lax.axis_index("col")
@@ -83,6 +83,11 @@
     target = 2 * r + c // 8
     self_row = jnp.where(target == c, r, -1)
 
+    pairs = [(fam_in, fam), (pair_in, pair), (wh_in, wh), (wo_in, wo), (wv_in, wv), (wvo_in, wvo), (wz_in, wz)]
+    loads = [pltpu.make_async_copy(a, b, in_s.at[i]) for i, (a, b) in enumerate(pairs)]
+    for cp in loads:
+        cp.start()
+
     def wrap(i, n):
         return lax.rem(i + n, n)
 
@@ -150,17 +155,19 @@
         if i == 1:
             return bc(1, 0, 0, 0, 4, 3, 0)
         if i == 2:
-            return bc(2, 3, 0, 0, 2, 1, 0)
+            return bc(2, 0, 0, 0, 4, 2, 0)
         if i == 3:
-            return bc(3, 1, 0, 2, 2, 3, 0)
+            return bc(3, 2, 0, 0, 4, 0, 2)
         dp = along[(i - 4) % 4]
         if i < 8:
             return bc(i, dp, 0, 0, 4, 0, 1)
         if i < 12:
             return bc(i, dp, 0, 0, 4, 0, 3)
-        if i < 16:
+        if i < 15:
             return bc(i, dp, 3, 0, 2, 0, 1)
         return bc(i, dp, 1, 2, 2, 0, 3)
+
+    b_used = [i for i in range(19) if i != 15]
 
     def b_core(dp, dq):
         ref = bref(dp, dq, 0, 4)
@@ -180,6 +187,7 @@
             b_core(*p).start()
 
     livr[r] = (present[...] * valid[pl.ds(r, 1), :]).astype(F32)
+    loads[0].wait()
     ft[zl] = fam[pl.ds(4 * zl, 4)]
     for s in range(4):
         nall[x, zl, s] = norm(ft[zl, s].astype(F32)).astype(BF)
@@ -204,18 +212,30 @@
             bscr[pl.ds(t * 64 + i * 8, 8), :] = b[:, i * 128:(i + 1) * 128]
         return carry
 
+    loads[1].wait()
     lax.fori_loop(0, 8, bias_step, 0)
     for h in range(H):
         mine[h] = bscr[pl.ds(h, 64, stride=8), :].astype(BF)
     sib_copy = copy(mine, sib, sb_s, sb_r, r, cs)
     sib_copy.start()
 
-    for g in range(G):
+    def pass_on(g, i):
+        for k in (i, i + 1):
+            nc(g, k).wait_recv()
+        for k in (i + 4, i + 5):
+            nc(g, k).start()
+
+    def partner(g):
         zc(g).wait_recv()
         for s in (2 * g, 2 * g + 1):
             nall[x, 1 - zl, s] = norm(ft[1 - zl, s].astype(F32)).astype(BF)
         for i in (2, 3):
             nc(g, i).start()
+
+    def query(zb, s):
+        rows = nall[x, zb, s]
+        qs[s, pl.ds(pl.multiple_of(zb * R, R), R), :] = (dot(rows, wh[0]) * (HD ** -0.5)).astype(BF)
+        gs[s, pl.ds(pl.multiple_of(zb * R, R), R), :] = sigmoid(dot(rows, wh[3]))
 
     sib_copy.wait_recv()
     low = lax.broadcasted_iota(jnp.int32, (64, 128), 1) < 64
@@ -226,33 +246,33 @@
         right_part = jnp.where(first, b, a)
         ball[zl, blk, h, 0:64, :] = jnp.where(low, left_part, pltpu.roll(right_part, 64, 1)).astype(BF)
         ball[zl, blk, h, 64:128, :] = jnp.where(low, pltpu.roll(left_part, 64, 1), right_part).astype(BF)
-    b_start(0, 1, 4, 8)
-
-    def pass_on(g, i):
-        for k in (i, i + 1):
-            nc(g, k).wait_recv()
-        for k in (i + 4, i + 5):
-            nc(g, k).start()
-
+    b_start(0, 1, 2, 4, 8)
+    partner(0)
+    partner(1)
+    loads[2].wait()
+    query(zl, 0)
     pass_on(0, 0)
-
-    for zb in range(2):
-        for s in range(4):
-            rows = nall[x, zb, s]
-            qs[s, zb * R:(zb + 1) * R, :] = (dot(rows, wh[0]) * (HD ** -0.5)).astype(BF)
-            gs[s, zb * R:(zb + 1) * R, :] = sigmoid(dot(rows, wh[3]))
-
     b_wait(0, 1)
-    b_start(2, 3, 5, 9, 6, 10)
+    b_start(5, 9, 6, 10)
     b_swap((3, 0), (1, 0))
-    pass_on(0, 2)
+    b_wait(2)
+    b_start(7, 11, 3)
+    b_swap((2, 0))
+    query(zl, 1)
     b_wait(4, 8)
     b_start(12, 16)
     b_swap((0, 3), (0, 1))
+    pass_on(0, 2)
+    query(zl, 2)
     pass_on(1, 0)
-    b_wait(2, 3)
-    b_start(7, 11)
-    b_swap((2, 0))
+    query(zl, 3)
+    b_wait(5, 9)
+    b_start(13, 17)
+    b_swap((3, 3), (3, 1))
+    query(1 - zl, 0)
+    b_wait(6, 10)
+    b_start(14, 18)
+    b_swap((1, 3), (1, 1))
     pass_on(1, 2)
 
     for k in range(1, NR):
@@ -271,23 +291,12 @@
         lr(k).start()
         lc(k).start()
 
-    b_wait(5, 9)
-    b_start(13, 17)
-    b_swap((3, 3), (3, 1))
-    b_wait(6, 10)
-    b_start(14, 18)
-    b_swap((1, 3), (1, 1))
+    for s in (1, 2, 3):
+        query(1 - zl, s)
     b_wait(12, 16)
     b_swap((0, 2))
     b_wait(7, 11)
-    b_start(15, 19)
     b_swap((2, 3), (2, 1))
-    b_wait(13, 17)
-    b_swap((3, 2))
-    b_wait(14, 18)
-    b_swap((1, 2))
-    b_wait(15, 19)
-    b_swap((2, 2))
 
     def keys_values(g):
         for i in (4, 5, 6, 7):
@@ -299,6 +308,13 @@
                 vs[s, b * R:(b + 1) * R, :] = dot(rows, wh[2]).astype(BF)
 
     keys_values(0)
+    b_wait(13, 17)
+    b_swap((3, 2))
+    b_wait(14, 18)
+    b_swap((1, 2))
+    b_wait(3)
+    b_swap((2, 2))
+    loads[3].wait()
     for i in range(1, 16):
         b_core(i // 4, i % 4).wait_recv()
 
@@ -350,6 +366,8 @@
     ltt[...] = lcol[...].reshape(R, R).T
     right_live = ltt[pl.ds(pl.multiple_of(core * 64, 64), 64), :]
     inv[...] = 1.0 / jnp.maximum(dot_t(right_live.astype(BF), by_res.astype(BF)), 1.0)
+    for i in (4, 5, 6):
+        loads[i].wait()
     wzt[...] = wz[...].astype(F32).T.astype(BF)
     for g in range(G):
         for k in range(NC):
@@ -404,26 +422,15 @@
         lrcv[c, p * 128:(p + 1) * 128, :] = lf[p * 128:(p + 1) * 128, :].astype(BF)
         rsnd[p * 128:(p + 1) * 128, :] = rf[p * 128:(p + 1) * 128, :].astype(BF)
 
-    cz = c + 2 - 4 * zh
-    cl, cr = wrap(c + 12, NC), wrap(c + 4, NC)
-
-    def far(i):
-        return i + 2 - 4 * lax.rem(i // 2, 2)
-
-    l_plan = [
-        (c, 0, 128, cz), (c, 0, 128, cr), (c, 0, 128, cl), (far(c), 0, 128, cr), (far(c), 0, 128, cl),
-        (cl, 0, 64, cr), (cr, 64, 64, cl), (far(cl), 0, 64, cr), (far(cr), 64, 64, cl),
-    ]
-    near = lax.rem(far(c) - c + NC, NC) // 2
-
-    def lslot(p, i):
-        owner, lo, n, to = l_plan[i]
-        ref = lrcv.at[owner, pl.ds(p * 128 + lo, n)]
-        return copy(ref, ref, le_s.at[p, i], le_r.at[p, i], r, to)
-
-    def lswap(p, i):
-        ref = lrcv.at[wrap(c + 2 * i, NC), pl.ds(p * 128, 128)]
-        return copy(ref, ref, lw_s.at[p, i], lw_r.at[p, i], r, cs)
+    def lslot(p, k):
+        ref = lrcv.at[c, pl.ds(p * 128, 128)]
+        return copy(ref, ref, le_s.at[p, k], le_r.at[p, k], r, wrap(c + 2 * k, NC))
+
+    def lswap(p, k):
+        ref = lrcv.at[wrap(c - 2 * k, NC), pl.ds(p * 128, 128)]
+        return copy(ref, ref, lw_s.at[p, k], lw_r.at[p, k], r, cs)
+
+    near_first = (2, 6, 4, 1, 7, 3, 5)
 
     place = lax.rem(c, 8)
 
@@ -431,35 +438,15 @@
         span = pl.ds(p * 128, 128)
         return copy(rsnd.at[span], rrcv.at[place, span], ri_s.at[p, k], ri_r.at[p, place], k, target)
 
-    def left_one(p):
-        for i in (0, 1, 2):
-            lslot(p, i).start()
+    def left_send(p):
+        for k in near_first:
+            lslot(p, k).start()
         lswap(p, 0).start()
 
-    def left_two(p):
-        for i in (0, 1, 2):
-            lslot(p, i).wait_recv()
-        for i in (3, 4, 5, 6):
-            lslot(p, i).start()
-        lswap(p, near).start()
-        lswap(p, 2).start()
-        lswap(p, 6).start()
-
-    def left_three(p):
-        for i in (3, 4):
-            lslot(p, i).wait_recv()
-        for i in (7, 8):
-            lslot(p, i).start()
-        lswap(p, lax.rem(near + 2, 8)).start()
-        lswap(p, lax.rem(near + 6, 8)).start()
-        for i in (5, 6):
-            lslot(p, i).wait_recv()
-        lswap(p, 4).start()
-
-    def left_four(p):
-        for i in (7, 8):
-            lslot(p, i).wait_recv()
-        lswap(p, lax.rem(near + 4, 8)).start()
+    def left_swap(p):
+        for k in near_first:
+            lslot(p, k).wait_recv()
+            lswap(p, k).start()
 
     def right_send(p):
         for k in range(8):
@@ -475,23 +462,16 @@
                 copy(rsnd.at[span], rrcv.at[k, span], ri_s.at[p, k], ri_r.at[p, k], r, c).wait_recv()
 
     col_half(0)
-    left_one(0)
+    left_send(0)
     right_send(0)
     col_half(1)
-    left_one(1)
-    left_two(0)
-    left_two(1)
-    left_three(0)
-    left_three(1)
+    left_send(1)
     right_send(1)
 
     @pl.when(target == c)
     def _():
         rrcv[place] = rsnd[...]
 
-    left_four(0)
-    left_four(1)
-
     for i in range(2):
         back_snd[:, :, i * 128:(i + 1) * 128] = upf[i].reshape(NC, 64, 128).astype(BF)
 
@@ -499,10 +479,31 @@
         to = wrap(c + k, NC)
         return copy(back_snd.at[to], back_rcv.at[c], u_s.at[k], u_r.at[k], r, to)
 
+    sib_copy.wait_send()
+    for g in range(G):
+        zc(g).wait_send()
+    for g in range(G):
+        for i in range(8):
+            nc(g, i).wait_send()
+        for k in range(NC):
+            mc(g, 1 - zl, k).wait_send()
+            if k > 0:
+                mc(g, zl, k).wait_send()
+    for k in range(1, NR):
+        lv(k).wait_send()
+    for k in range(1, NC):
+        lr(k).wait_send()
+        lc(k).wait_send()
+    for i in b_used:
+        b_slot(i).wait_send()
+    for i in range(1, 16):
+        b_core(i // 4, i % 4).wait_send()
+
+    left_swap(0)
+    left_swap(1)
     for k in range(1, NC):
         uc(k).start()
     back_rcv[c] = back_snd[c]
-
     for p in range(2):
         for i in range(8):
             lswap(p, i).wait_recv()
@@ -564,29 +565,11 @@
     out_copy(2).wait()
     out_copy(3).wait()
 
-    for g in range(G):
-        zc(g).wait_send()
-    sib_copy.wait_send()
-    for g in range(G):
-        for i in range(8):
-            nc(g, i).wait_send()
-        for k in range(NC):
-            mc(g, 1 - zl, k).wait_send()
-            if k > 0:
-                mc(g, zl, k).wait_send()
-    for k in range(1, NR):
-        lv(k).wait_send()
     for k in range(1, NC):
-        lr(k).wait_send()
-        lc(k).wait_send()
         uc(k).wait_send()
-    for i in range(20):
-        b_slot(i).wait_send()
-    for i in range(1, 16):
-        b_core(i // 4, i % 4).wait_send()
     for p in range(2):
-        for i in range(9):
-            lslot(p, i).wait_send()
+        for k in near_first:
+            lslot(p, k).wait_send()
         for i in range(8):
             lswap(p, i).wait_send()
         for k in range(8):
@@ -595,25 +578,36 @@
                 rcopy(p, k).wait_send()
 
 
-def relay_kernel(a, b, a_out, b_out, sem):
-    copies = [pltpu.make_async_copy(a, a_out, sem.at[0])]
-    for i in range(4):
-        rows = pl.ds(i * 32, 32)
-        copies.append(pltpu.make_async_copy(b.at[rows], b_out.at[rows], sem.at[1 + i]))
-    for cp in copies:
+def relay_kernel(a, b, a_out, b_out, a_mid, b_mid, sem):
+    refs = [(a, a_mid, a_out, pl.ds(0, S))]
+    refs += [(b, b_mid, b_out, pl.ds(i * 32, 32)) for i in range(4)]
+    into = [pltpu.make_async_copy(p.at[rows], q.at[rows], sem.at[0, i]) for i, (p, q, _, rows) in enumerate(refs)]
+    back = [pltpu.make_async_copy(q.at[rows], o.at[rows], sem.at[1, i]) for i, (_, q, o, rows) in enumerate(refs)]
+    for cp in into:
         cp.start()
-    for cp in copies:
+    for one, two in zip(into, back):
+        one.wait()
+        two.start()
+    for cp in back:
         cp.wait()
 
 
 def per_device(fam, pair, present, valid, wh, wo, wb, wv, wvo, wlr, wz):
     vm = pl.BlockSpec(memory_space=pltpu.VMEM)
+    anywhere = pl.BlockSpec(memory_space=pl.ANY)
     dma = pltpu.SemaphoreType.DMA
 
     def sems(*shape):
         return [dma(shape), dma(shape)]
 
     scratch = [
+        pltpu.VMEM((S, R, D), BF),
+        pltpu.VMEM((R, 64, 128), BF),
+        pltpu.VMEM((4, D, D), BF),
+        pltpu.VMEM((D, D), BF),
+        pltpu.VMEM((4, D, D), BF),
+        pltpu.VMEM((D, D), BF),
+        pltpu.VMEM((1024, 128), BF),
         pltpu.VMEM((2, 4, R, D), BF),
         pltpu.VMEM((4, 2, 4, R, D), BF),
         pltpu.VMEM((NR, S, R), F32),
@@ -653,12 +647,12 @@
         pltpu.VMEM((R * 64, 128), F32),
         pltpu.VMEM((2, R, 16, 128), BF),
         *sems(G), *sems(G, 8), *sems(8), *sems(16), *sems(16), dma, dma, *sems(20), *sems(15),
-        *sems(G, 2, 16), *sems(16), *sems(2, 9), *sems(2, 8), *sems(2, 8), dma((2,)),
+        *sems(G, 2, 16), *sems(16), *sems(2, 8), *sems(2, 8), *sems(2, 8), dma((2,)), dma((7,)),
     ]
     align, pair_out = pl.pallas_call(
         msa_kernel,
         out_shape=(jax.ShapeDtypeStruct((S, R, D), BF), jax.ShapeDtypeStruct((R, 64, 128), BF)),
-        in_specs=[vm] * 11,
+        in_specs=[anywhere, anywhere, vm, vm, anywhere, anywhere, vm, anywhere, anywhere, vm, anywhere],
         out_specs=(vm, pl.BlockSpec(memory_space=pl.ANY)),
         scratch_shapes=scratch,
         compiler_params=pltpu.CompilerParams(
@@ -669,13 +663,12 @@
         fam, pair, present, valid.reshape(NR, R), wh, wo, wb.T, wv, wvo,
         wlr.transpose(0, 2, 1).reshape(64, D), wz,
     )
-    anywhere = pl.BlockSpec(memory_space=pl.ANY)
     return pl.pallas_call(
         relay_kernel,
         out_shape=(jax.ShapeDtypeStruct((S, R, D), BF), jax.ShapeDtypeStruct((R, 64, 128), BF)),
         in_specs=[anywhere] * 2,
         out_specs=(anywhere,) * 2,
-        scratch_shapes=[dma((5,))],
+        scratch_shapes=[pltpu.VMEM((S, R, D), BF), pltpu.VMEM((R, 64, 128), BF), dma((2, 5))],
         compiler_params=pltpu.CompilerParams(vmem_limit_bytes=60 * 1024 * 1024),
         name="relay",
     )(align, pair_out)

time: 181 us -> 97.3 us (0.54)
  Pallas kernels: 179 us -> 96.3 us
    pallas_call x1, Pallas kernels: 80.6 us -> 2.61 us  [per_device(): pl.pallas_call(relay_kernel, out_shape=(jax.ShapeDtypeStruct((S, R, D), B...]
    pallas_call x1, Pallas kernels: 98.9 us -> 93.7 us  [per_device(): pl.pallas_call(msa_kernel, out_shape=(jax.ShapeDtypeStruct((S, R, D), BF)...]
where the time goes in v4:
time: 97.3 us; the launch traced here: 97.1 us
  Pallas kernels  96.3 us (99%)
    pallas_call x1, Pallas kernels, per_device(): pl.pallas_call(msa_kernel, out_shape=(jax.ShapeDtypeStruct((S, R, D), BF)...  93.7 us
    pallas_call x1, Pallas kernels, per_device(): pl.pallas_call(relay_kernel, out_shape=(jax.ShapeDtypeStruct((S, R, D), B...  2.61 us

profile of v4, /device:TPU:1, one launch (start us, length us, event | category | flops | bytes accessed | tf_op | source)
XLA Modules:
  0.0 97.1 jit_solution(452004856570959198)
XLA Ops:
  0.6 93.7 %msa.1 = (bf16[8,128,256]{2,1,0:T(8,128)(2,1)}, bf16[128,64,128]{2,1,0:T(8,128)(2,1)}) custom-call(bf16[8,128,256]{2,1,0:T(8,128)(2,1)} %fam_in.1, bf16[128,64,128]{2,1,0:T(8,128)(2,1)} %pair_in.1, s32[8,128]{1,0:T(8,128)} %present.1, s32[8,128]{1,0:T(8,128)} %bitcast.6, bf16[4,256,256]{2,1,0:T(8,128)(2,1)} %wh_in.1, bf16[256,256]{1,0:T(8,128)(2,1)} %wo_in.1, ...), custom_call_target="tpu_custom_call" | custom-call | tf_op jit(solution)/shard_map/msa/pallas_call | solution.py:652
  94.3 2.6 %relay.1 = (bf16[8,128,256]{2,1,0:T(8,128)(2,1)}, bf16[128,64,128]{2,1,0:T(8,128)(2,1)}) custom-call(bf16[8,128,256]{2,1,0:T(8,128)(2,1)} %get-tuple-element.4.a, bf16[128,64,128]{2,1,0:T(8,128)(2,1)} %get-tuple-element.5.b), custom_call_target="tpu_custom_call" | custom-call | tf_op jit(solution)/shard_map/relay/pallas_call | solution.py:666

commit v5 on v4

--- a/solution.py
+++ b/solution.py
@@ -147,6 +147,7 @@
         ref = bref(dp, dq, lo, n)
         return copy(ref, ref, b_s.at[slot], b_r.at[slot], 2 * x + lax.rem(tz, 2), 4 * ty + 2 * (tz // 2) + core)
 
+    in_pair, out_pair = 1 + 2 * zl, 3 - 2 * zl
     along = (0, 3, 1, 2)
 
     def b_slot(i):
@@ -164,8 +165,8 @@
         if i < 12:
             return bc(i, dp, 0, 0, 4, 0, 3)
         if i < 15:
-            return bc(i, dp, 3, 0, 2, 0, 1)
-        return bc(i, dp, 1, 2, 2, 0, 3)
+            return bc(i, dp, jnp.where(first, 3, in_pair), 0, 2, 0, jnp.where(first, 1, out_pair))
+        return bc(i, dp, jnp.where(first, 1, in_pair), 2, 2, 0, jnp.where(first, 3, out_pair))
 
     b_used = [i for i in range(19) if i != 15]
 
@@ -189,11 +190,12 @@
     livr[r] = (present[...] * valid[pl.ds(r, 1), :]).astype(F32)
     loads[0].wait()
     ft[zl] = fam[pl.ds(4 * zl, 4)]
-    for s in range(4):
-        nall[x, zl, s] = norm(ft[zl, s].astype(F32)).astype(BF)
     pl.semaphore_wait(barrier, jnp.where(target == c, 51, 53))
     for g in range(G):
         zc(g).start()
+    for g in range(G):
+        for s in (2 * g, 2 * g + 1):
+            nall[x, zl, s] = norm(ft[zl, s].astype(F32)).astype(BF)
         for i in (0, 1):
             nc(g, i).start()
 
@@ -204,16 +206,18 @@
         lv(k).start()
 
     def bias_step(t, carry):
-        lo = pair[pl.ds(t * 8, 8)].astype(F32)
-        hi = pair[pl.ds(64 + t * 8, 8)].astype(F32)
-        rows = norm(jnp.concatenate([lo, hi], axis=1).reshape(1024, 128)).astype(BF)
+        lo = pair[pl.ds(t * 8, 8)]
+        hi = pair[pl.ds(64 + t * 8, 8)]
+        both = jnp.concatenate([lo, hi], axis=1).reshape(1024, 128)
+        off = both.astype(F32) - dot(both, jnp.full((128, 128), 1 / 128, BF))
+        rows = (off * lax.rsqrt(jnp.mean(off * off, axis=-1, keepdims=True) + EPS)).astype(BF)
         b = dot_t(wb[...], rows)
         for i in range(8):
             bscr[pl.ds(t * 64 + i * 8, 8), :] = b[:, i * 128:(i + 1) * 128]
         return carry
 
     loads[1].wait()
-    lax.fori_loop(0, 8, bias_step, 0)
+    lax.fori_loop(0, 8, bias_step, 0, unroll=8)
     for h in range(H):
         mine[h] = bscr[pl.ds(h, 64, stride=8), :].astype(BF)
     sib_copy = copy(mine, sib, sb_s, sb_r, r, cs)
@@ -374,17 +378,14 @@
             mc(g, 1 - zl, k).wait_recv()
             if k > 0:
                 mc(g, zl, k).wait_recv()
-
-    def col_norm(t, carry):
-        mid = rcv[t].reshape(64, D).astype(F32)
-        rows = pl.ds(pl.multiple_of(t * 64, 64), 64)
-        normed = norm(mid)
-        for i in range(2):
-            xf[i, rows, :] = mid[:, i * 128:(i + 1) * 128]
-            nf[i, rows, :] = normed[:, i * 128:(i + 1) * 128]
-        return carry
-
-    lax.fori_loop(0, NC, col_norm, 0)
+        for t in range(0, NC, 4):
+            mid = rcv[t:t + 4, :, g * 16:(g + 1) * 16, :].reshape(128, D).astype(F32)
+            normed = norm(mid)
+            for u in range(8):
+                to = slice(t * 64 + u * 32 + g * 16, t * 64 + u * 32 + g * 16 + 16)
+                for i in range(2):
+                    xf[i, to, :] = mid[u * 16:(u + 1) * 16, i * 128:(i + 1) * 128]
+                    nf[i, to, :] = normed[u * 16:(u + 1) * 16, i * 128:(i + 1) * 128]
 
     def rows_of(ref, p):
         return jnp.concatenate(
@@ -466,7 +467,6 @@
     right_send(0)
     col_half(1)
     left_send(1)
-    right_send(1)
 
     @pl.when(target == c)
     def _():
@@ -500,6 +500,7 @@
         b_core(i // 4, i % 4).wait_send()
 
     left_swap(0)
+    right_send(1)
     left_swap(1)
     for k in range(1, NC):
         uc(k).start()
@@ -515,14 +516,12 @@
         ltall[(2 * m + 1) * R:(2 * m + 2) * R, :] = jnp.where(low4, pltpu.roll(a, R - 4, 0), b).astype(BF)
 
     def out_copy(q):
-        return pltpu.make_async_copy(
-            blocks.at[lax.rem(q, 2)], pair_out.at[:, pl.ds(pl.multiple_of(q * 16, 16), 16), :], o_s.at[lax.rem(q, 2)]
-        )
-
-    def eight(q, p):
-        rows = jnp.concatenate([rrcv[2 * q + t, p * 128:(p + 1) * 128, :] for t in range(2)], axis=0)
+        return pltpu.make_async_copy(blocks.at[q], pair_out.at[:, pl.ds(q * 16, 16), :], o_s.at[q])
+
+    def sixteen(q, p):
+        rows = jnp.concatenate([rrcv[4 * q + t, p * 128:(p + 1) * 128, :] for t in range(4)], axis=0)
         o = dot_t(rows, ltall[...]).astype(BF)
-        for j0 in range(0, 8, 2):
+        for j0 in range(0, 16, 2):
             two = jnp.concatenate(
                 [
                     jnp.concatenate([o[j * HD:(j + 1) * HD, i * R:(i + 1) * R] for i in range(HD)], axis=0)
@@ -532,38 +531,28 @@
             )
             prod = dot(wzt[...], two)
             for i in range(2):
-                j = q * 16 + (j0 + i) // NB * 8 + p * NB + (j0 + i) % NB
+                j = q * 32 + (j0 + i) // NB * 8 + p * NB + (j0 + i) % NB
                 one = prod[:, i * R:(i + 1) * R] * inv[pl.ds(j, 1), :]
                 acc[pl.ds(j, R, stride=64), :] = one.T
 
     def first_half(q, carry):
-        eight(q, 0)
+        sixteen(q, 0)
         return carry
 
-    def second_half(q, carry):
-        eight(q, 1)
-
-        @pl.when(q >= 2)
-        def _():
-            out_copy(q - 2).wait()
-
-        for t in range(4):
-            @pl.when(q == t)
-            def _():
-                blocks[t % 2] = acc[...].reshape(R, 64, 128)[:, t * 16:(t + 1) * 16, :].astype(BF)
-        out_copy(q).start()
-        return carry
-
     right_wait(0)
-    lax.fori_loop(0, 4, first_half, 0)
+    lax.fori_loop(0, 2, first_half, 0)
     right_wait(1)
-    lax.fori_loop(0, 4, second_half, 0)
+    for q in range(2):
+        sixteen(q, 1)
+        for t in (2 * q, 2 * q + 1):
+            blocks[t] = acc[...].reshape(R, 64, 128)[:, t * 16:(t + 1) * 16, :].astype(BF)
+            out_copy(t).start()
     for k in range(1, NC):
         uc(k).wait_recv()
     for s in range(S):
         align[s] = jnp.concatenate([back_rcv[t, s * 8:(s + 1) * 8, :] for t in range(NC)], axis=0)
-    out_copy(2).wait()
-    out_copy(3).wait()
+    for q in range(4):
+        out_copy(q).wait()
 
     for k in range(1, NC):
         uc(k).wait_send()
@@ -645,9 +634,9 @@
         pltpu.VMEM((HD * R, 128), BF),
         pltpu.VMEM((128, 1024), BF),
         pltpu.VMEM((R * 64, 128), F32),
-        pltpu.VMEM((2, R, 16, 128), BF),
+        pltpu.VMEM((4, R, 16, 128), BF),
         *sems(G), *sems(G, 8), *sems(8), *sems(16), *sems(16), dma, dma, *sems(20), *sems(15),
-        *sems(G, 2, 16), *sems(16), *sems(2, 8), *sems(2, 8), *sems(2, 8), dma((2,)), dma((7,)),
+        *sems(G, 2, 16), *sems(16), *sems(2, 8), *sems(2, 8), *sems(2, 8), dma((4,)), dma((7,)),
     ]
     align, pair_out = pl.pallas_call(
         msa_kernel,

time: 97.3 us -> 93 us (0.956)
  Pallas kernels: 96.3 us -> 91.9 us
    pallas_call x1, Pallas kernels: 93.7 us -> 89.3 us  [per_device(): pl.pallas_call(msa_kernel, out_shape=(jax.ShapeDtypeStruct((S, R, D), BF)...]
where the time goes in v5:
time: 93 us; the launch traced here: 92.7 us
  Pallas kernels  91.9 us (99%)
    pallas_call x1, Pallas kernels, per_device(): pl.pallas_call(msa_kernel, out_shape=(jax.ShapeDtypeStruct((S, R, D), BF)...  89.3 us
    pallas_call x1, Pallas kernels, per_device(): pl.pallas_call(relay_kernel, out_shape=(jax.ShapeDtypeStruct((S, R, D), B...  2.61 us

profile of v5, /device:TPU:1, one launch (start us, length us, event | category | flops | bytes accessed | tf_op | source)
XLA Modules:
  0.0 92.7 jit_solution(6697721973064124967)
XLA Ops:
  0.6 89.3 %msa.1 = (bf16[8,128,256]{2,1,0:T(8,128)(2,1)}, bf16[128,64,128]{2,1,0:T(8,128)(2,1)}) custom-call(bf16[8,128,256]{2,1,0:T(8,128)(2,1)} %fam_in.1, bf16[128,64,128]{2,1,0:T(8,128)(2,1)} %pair_in.1, s32[8,128]{1,0:T(8,128)} %present.1, s32[8,128]{1,0:T(8,128)} %bitcast.6, bf16[4,256,256]{2,1,0:T(8,128)(2,1)} %wh_in.1, bf16[256,256]{1,0:T(8,128)(2,1)} %wo_in.1, ...), custom_call_target="tpu_custom_call" | custom-call | tf_op jit(solution)/shard_map/msa/pallas_call | solution.py:641
  89.9 2.6 %relay.1 = (bf16[8,128,256]{2,1,0:T(8,128)(2,1)}, bf16[128,64,128]{2,1,0:T(8,128)(2,1)}) custom-call(bf16[8,128,256]{2,1,0:T(8,128)(2,1)} %get-tuple-element.4.a, bf16[128,64,128]{2,1,0:T(8,128)(2,1)} %get-tuple-element.5.b), custom_call_target="tpu_custom_call" | custom-call | tf_op jit(solution)/shard_map/relay/pallas_call | solution.py:655

commit v6 on v5

--- a/solution.py
+++ b/solution.py
@@ -472,12 +472,15 @@
     def _():
         rrcv[place] = rsnd[...]
 
-    for i in range(2):
-        back_snd[:, :, i * 128:(i + 1) * 128] = upf[i].reshape(NC, 64, 128).astype(BF)
-
     def uc(k):
         to = wrap(c + k, NC)
         return copy(back_snd.at[to], back_rcv.at[c], u_s.at[k], u_r.at[k], r, to)
+
+    left_swap(0)
+    right_send(1)
+
+    for i in range(2):
+        back_snd[:, :, i * 128:(i + 1) * 128] = upf[i].reshape(NC, 64, 128).astype(BF)
 
     sib_copy.wait_send()
     for g in range(G):
@@ -499,8 +502,6 @@
     for i in range(1, 16):
         b_core(i // 4, i % 4).wait_send()
 
-    left_swap(0)
-    right_send(1)
     left_swap(1)
     for k in range(1, NC):
         uc(k).start()
@@ -540,7 +541,7 @@
         return carry
 
     right_wait(0)
-    lax.fori_loop(0, 2, first_half, 0)
+    lax.fori_loop(0, 2, first_half, 0, unroll=2)
     right_wait(1)
     for q in range(2):
         sixteen(q, 1)

time: 93 us -> 92.5 us (level)
  no operation moved by 1% of the time
where the time goes in v6:
time: 92.5 us; the launch traced here: 92.3 us
  Pallas kernels  91.4 us (99%)
    pallas_call x1, Pallas kernels, per_device(): pl.pallas_call(msa_kernel, out_shape=(jax.ShapeDtypeStruct((S, R, D), BF)...  88.8 us
    pallas_call x1, Pallas kernels, per_device(): pl.pallas_call(relay_kernel, out_shape=(jax.ShapeDtypeStruct((S, R, D), B...  2.61 us

profile of v6, /device:TPU:1, one launch (start us, length us, event | category | flops | bytes accessed | tf_op | source)
XLA Modules:
  0.0 92.3 jit_solution(5471844932771369089)
XLA Ops:
  0.6 88.8 %msa.1 = (bf16[8,128,256]{2,1,0:T(8,128)(2,1)}, bf16[128,64,128]{2,1,0:T(8,128)(2,1)}) custom-call(bf16[8,128,256]{2,1,0:T(8,128)(2,1)} %fam_in.1, bf16[128,64,128]{2,1,0:T(8,128)(2,1)} %pair_in.1, s32[8,128]{1,0:T(8,128)} %present.1, s32[8,128]{1,0:T(8,128)} %bitcast.6, bf16[4,256,256]{2,1,0:T(8,128)(2,1)} %wh_in.1, bf16[256,256]{1,0:T(8,128)(2,1)} %wo_in.1, ...), custom_call_target="tpu_custom_call" | custom-call | tf_op jit(solution)/shard_map/msa/pallas_call | solution.py:642
  89.5 2.6 %relay.1 = (bf16[8,128,256]{2,1,0:T(8,128)(2,1)}, bf16[128,64,128]{2,1,0:T(8,128)(2,1)}) custom-call(bf16[8,128,256]{2,1,0:T(8,128)(2,1)} %get-tuple-element.4.a, bf16[128,64,128]{2,1,0:T(8,128)(2,1)} %get-tuple-element.5.b), custom_call_target="tpu_custom_call" | custom-call | tf_op jit(solution)/shard_map/relay/pallas_call | solution.py:656
